TPU v7x, 128 devices: a whole 4x4x4 slice. The times are simulated.
128 devices in a mesh: row: 8 (over z_lo, y), col: 16 (over z_hi, x, core).
Axes of the slice: x: 4, y: 4, z: 4 (z_hi: 2, z_lo: 2; z = z_hi * 2 + z_lo), core: 2. Of those that a mesh axis runs over, the one named last changes fastest.
Arguments:
- activations: bfloat16 [768, 8192], P('col', 'row'), may hold values from -6 to 6
- out_grad: bfloat16 [768, 8192], P('col', 'row'), may hold values from -3 to 3
- w_gate: bfloat16 [8192, 26624], P('row', 'col'), may hold values from -0.0625 to 0.0625
- w_up: bfloat16 [8192, 26624], P('row', 'col'), may hold values from -0.0625 to 0.0625
- w_down: bfloat16 [26624, 8192], P('col', 'row'), may hold values from -0.0390625 to 0.0390625
Outputs:
- input_grad: bfloat16 [768, 8192], P('col', 'row')
- gate_grad: bfloat16 [8192, 26624], P('row', 'col')
- up_grad: bfloat16 [8192, 26624], P('row', 'col')
- down_grad: bfloat16 [26624, 8192], P('col', 'row')
All inputs are finite; a program needn't handle non-finite values.
Results may differ from a plain program's by a relative error of at most 0.005.
Values may be sent and summed in bfloat16 or wider, within the bound.
A program may use at most 128 MiB of HBM per device.

v0:
```python
import jax
import jax.numpy as jnp
from jax import lax
from jax.sharding import PartitionSpec as P


def contract_first(left, right):
    return lax.dot_general(
        left, right, (((0,), (0,)), ((), ())), preferred_element_type=jnp.float32
    )


def contract_last(left, right):
    return lax.dot_general(
        left, right, (((1,), (1,)), ((), ())), preferred_element_type=jnp.float32
    )


def swiglu_back(gate, upper, hidden_grad):
    sig = jax.nn.sigmoid(gate)
    act = gate * sig
    hidden = (act * upper).astype(jnp.bfloat16)
    gate_delta = (hidden_grad * upper * sig * (1.0 + gate * (1.0 - sig))).astype(jnp.bfloat16)
    up_delta = (hidden_grad * act).astype(jnp.bfloat16)
    return (hidden, gate_delta, up_delta)


def per_device(activations, out_grad, w_gate, w_up, w_down):
    act_all, grad_all = (
        lax.all_gather(activations, "col", axis=0, tiled=True),
        lax.all_gather(out_grad, "col", axis=0, tiled=True),
    )
    gate_part = jnp.dot(act_all, w_gate, preferred_element_type=jnp.float32)
    upper_part = jnp.dot(act_all, w_up, preferred_element_type=jnp.float32)
    hgrad_part = contract_last(grad_all, w_down)
    gate, upper, hidden_grad = lax.psum((gate_part, upper_part, hgrad_part), "row")
    hidden, gate_delta, up_delta = swiglu_back(gate, upper, hidden_grad)
    gate_grad = contract_first(act_all, gate_delta).astype(jnp.bfloat16)
    up_grad = contract_first(act_all, up_delta).astype(jnp.bfloat16)
    down_grad = contract_first(hidden, grad_all).astype(jnp.bfloat16)
    input_grad = lax.psum_scatter(
        contract_last(gate_delta, w_gate) + contract_last(up_delta, w_up),
        "col",
        scatter_dimension=0,
        tiled=True,
    ).astype(jnp.bfloat16)
    return (input_grad, gate_grad, up_grad, down_grad)


def solution(mesh):
    placed = (P("col", "row"), P("col", "row"), P("row", "col"), P("row", "col"), P("col", "row"))
    return jax.shard_map(
        per_device,
        mesh=mesh,
        in_specs=placed,
        out_specs=(P("col", "row"), P("row", "col"), P("row", "col"), P("col", "row")),
        check_vma=False,
    )
```

profile of v0, /device:TPU:0, one launch (start us, length us, event | category | flops | bytes accessed | tf_op | source)
XLA Modules:
  0.0 528.2 jit_solution(13659814859521011462)
XLA Ops:
  7.2 0.0 copy-start
  7.2 0.0 all-gather.5.cloned.1.call-start
  7.2 0.7 all-gather.5.cloned.1.call-update
  7.9 0.0 all-gather.3.cloned.1.call-start
  8.0 0.7 all-gather.3.cloned.1.call-update
  8.7 0.0 all-reduce.3.cloned.1.call-start
  8.7 51.1 %all-gather.5.cloned.1.call-done = bf16[768,1024]{1,0:T(8,128)(2,1)} async-done(((bf16[48,1024]{1,0:T(8,128)(2,1)}), bf16[768,1024]{1,0:T(8,128)(2,1)}) %all-gather.5.cloned.1.call-update) | async-done | bytes 1572880 | tf_op jit(solution)/shard_map/all_gather | solution.py:30
  59.8 0.0 copy-done
  59.8 0.0 copy-start.4
  59.8 0.0 copy-start.6
  59.8 6.8 %fusion.7 = f32[768,1664]{1,0:T(8,128)} fusion(bf16[768,1024]{1,0:T(8,128)(2,1)} %all-gather.5.cloned.1.call-done, bf16[1024,1664]{1,0:T(8,128)(2,1)S(1)} %copy-done), kind=kOutput, calls=%fused_computation.14 | convolution fusion | flops 2617245696 | bytes 10092544 | tf_op jit(solution)/shard_map/dot_general | solution.py:33
  66.6 0.0 copy-done.4
  66.6 0.0 copy-done.6
  66.6 4.8 fusion.6
  71.3 36.3 %all-gather.3.cloned.1.call-done = bf16[768,1024]{1,0:T(8,128)(2,1)} async-done(((bf16[48,1024]{1,0:T(8,128)(2,1)}), bf16[768,1024]{1,0:T(8,128)(2,1)}) %all-gather.3.cloned.1.call-update) | async-done | bytes 1572880 | tf_op jit(solution)/shard_map/all_gather | solution.py:31
  107.7 7.8 %fusion.5 = f32[768,1664]{1,0:T(8,128)} fusion(bf16[768,1024]{1,0:T(8,128)(2,1)} %all-gather.3.cloned.1.call-done, bf16[1664,1024]{1,0:T(8,128)(2,1)} %param.9), kind=kOutput, calls=%fused_computation.12 | convolution fusion | flops 2617245696 | bytes 10092544 | tf_op jit(solution)/shard_map/dot_general | solution.py:14
  115.5 0.0 all-reduce.3.cloned.1.call-update
  115.5 0.2 reduce-scatter.2.cloned.1.call-start
  115.7 314.6 %all-reduce.3.cloned.1.call-done = (f32[768,1664]{1,0:T(8,128)}, f32[768,1664]{1,0:T(8,128)}, f32[768,1664]{1,0:T(8,128)}) async-done(((f32[768,1664]{1,0:T(8,128)}, f32[768,1664]{1,0:T(8,128)}, f32[768,1664]{1,0:T(8,128)}), (f32[768,1664]{1,0:T(8,128)}, f32[768,1664]{1,0:T(8,128)}, f32[768,1664]{1,0:T(8,128)})) %all-reduce.3.cloned.1.call-update) | async-done | bytes 15335440 | tf_op jit(solution)/shard_map/psum | solution.py:36
  430.3 6.6 %multiply_convert_fusion.1 = (bf16[768,1664]{1,0:T(8,128)(2,1)S(1)}, bf16[768,1664]{1,0:T(8,128)(2,1)S(1)}) fusion(f32[768,1664]{1,0:T(8,128)} %get-tuple-element.9, f32[768,1664]{1,0:T(8,128)} %get-tuple-element.8, f32[768,1664]{1,0:T(8,128)} %get-tuple-element.10), kind=kLoop, calls=%fused_computation.1 | loop fusion | flops 16613376 | bytes 20447232 | tf_op jit(solution)/shard_map/convert_element_type | solution.py:24
  436.9 0.0 copy-start.3
  436.9 0.0 copy-start.2
  436.9 0.0 copy-start.5
  437.0 3.0 fusion.8
  440.0 0.0 copy-done.3
  440.0 0.0 copy-done.2
  440.0 0.7 copy-done.5
  440.8 4.8 convolution_add_fusion
  445.6 0.0 reduce-scatter.2.cloned.1.call-update
  445.6 5.0 fusion.1
  450.6 3.5 copy.9
  454.1 5.2 fusion.2
  459.3 3.5 copy.10
  462.8 0.0 copy-start.1
  462.8 9.7 %convolution_convert_fusion = bf16[1664,1024]{1,0:T(8,128)(2,1)} fusion(bf16[768,1024]{1,0:T(8,128)(2,1)} %all-gather.3.cloned.1.call-done, f32[768,1664]{1,0:T(8,128)} %get-tuple-element.10, f32[768,1664]{1,0:T(8,128)} %get-tuple-element.8), kind=kOutput, calls=%fused_computation.5 | convolution fusion | flops 2626617344 | bytes 15204352 | tf_op jit(solution)/shard_map/dot_general | solution.py:8
  472.5 47.6 %reduce-scatter.2.cloned.1.call-done = f32[48,1024]{1,0:T(8,128)} async-done(((f32[768,1024]{1,0:T(8,128)}), f32[48,1024]{1,0:T(8,128)}) %reduce-scatter.2.cloned.1.call-update) | async-done | bytes 196624 | tf_op jit(solution)/shard_map/reduce_scatter | solution.py:41
  520.1 1.6 convert_element_type.29
  521.6 0.0 copy-done.1
Async XLA Ops:
  7.2 52.6 %copy-start = (bf16[1024,1664]{1,0:T(8,128)(2,1)S(1)}, bf16[1024,1664]{1,0:T(8,128)(2,1)}, u32[]{:S(2)}) copy-start(bf16[1024,1664]{1,0:T(8,128)(2,1)} %param.7) | copy-start | bytes 10223620
  7.2 52.6 %all-gather.5.cloned.1.call-start = ((), (), s32[]{:S(2)}) async-start(), calls=%async_computation.2 | async-start | bytes 1671168 | tf_op jit(solution)/shard_map/all_gather | solution.py:30
  7.9 99.7 %all-gather.3.cloned.1.call-start = ((), (), s32[]{:S(2)}) async-start(), calls=%async_computation.1 | async-start | bytes 1671168 | tf_op jit(solution)/shard_map/all_gather | solution.py:31
  8.7 421.6 %all-reduce.3.cloned.1.call-start = ((), (), s32[]{:S(2)}) async-start(), calls=%async_computation.4 | async-start | bytes 30670848 | tf_op jit(solution)/shard_map/psum | solution.py:36
  59.8 6.8 %copy-start.4 = (bf16[1024,1664]{1,0:T(8,128)(2,1)S(1)}, bf16[1024,1664]{1,0:T(8,128)(2,1)}, u32[]{:S(2)}) copy-start(bf16[1024,1664]{1,0:T(8,128)(2,1)} %param.8) | copy-start | bytes 10223620
  59.8 6.8 %copy-start.6 = (bf16[768,1024]{1,0:T(8,128)(2,1)S(1)}, bf16[768,1024]{1,0:T(8,128)(2,1)}, u32[]{:S(2)}) copy-start(bf16[768,1024]{1,0:T(8,128)(2,1)} %all-gather.5.cloned.1.call-done) | copy-start | bytes 4718596
  115.5 404.6 %reduce-scatter.2.cloned.1.call-start = ((), (), s32[]{:S(2)}) async-start(), calls=%async_computation.3 | async-start | bytes 3342336 | tf_op jit(solution)/shard_map/reduce_scatter | solution.py:41
  436.9 3.1 copy-start.3
  436.9 3.1 copy-start.2
  436.9 3.8 copy-start.5
  462.8 58.8 %copy-start.1 = (bf16[1024,1664]{1,0:T(8,128)(2,1)S(1)}, bf16[1024,1664]{1,0:T(8,128)(2,1)}, u32[]{:S(2)}) copy-start(bf16[1024,1664]{1,0:T(8,128)(2,1)} %param.7) | copy-start | bytes 10223620
Sparse Core Ops, SparseCore 0:
  10.5 49.2 all-gather.4
  62.2 45.4 all-gather.2
  115.6 314.6 all-reduce.2
  445.7 74.3 reduce-scatter.1
where the time goes:
time: 528 us
  waiting for transfers between devices  451 us (85%)
  matrix products  47.1 us (9%)
  between operations  13.8 us (3%)
  other arithmetic  8.22 us (2%)
  local copies, waits for them, and re-layouts  7.78 us (1%)
    psum x1, waiting for transfers between devices, per_device(): lax.psum((gate_part, upper_part, hgrad_part), 'row')  315 us
    all_gather x1, waiting for transfers between devices, per_device(): lax.all_gather(activations, 'col', axis=0, tiled=True)  51.1 us
    reduce_scatter x1, waiting for transfers between devices, per_device(): lax.psum_scatter(contract_last(gate_delta, w_gate) + contract_last(up_del...  47.6 us
    all_gather x1, waiting for transfers between devices, per_device(): lax.all_gather(out_grad, 'col', axis=0, tiled=True)  36.3 us
    dot_general x3, matrix products, contract_first(): lax.dot_general(left, right, (((0,), (0,)), ((), ())), preferred_element_...  19.9 us
    dot_general x3, matrix products, contract_last(): lax.dot_general(left, right, (((1,), (1,)), ((), ())), preferred_element_...  15.6 us
  transfers between devices with their start and end apart: 4, of which 4 were waited for; matrix products, arithmetic and copies ran while one was open for 7% of the time, Pallas kernels for 0%

commit v1 on v0

v1 whole, which is shorter than its diff:
```python
import functools

import jax
import jax.numpy as jnp
from jax import lax
from jax.experimental import pallas as pl
from jax.experimental.pallas import tpu as pltpu
from jax.sharding import PartitionSpec as P

F32 = jnp.float32
BF16 = jnp.bfloat16
MESH = pl.DeviceIdType.MESH

CHUNKS = 6
CHUNK = 128
OWN = 16
D_LOCAL = 1024
H_LOCAL = 1664
TOKENS = 768
BLOCK = 48
SLOT = 192
WIDTH_A = 896
WIDTH_B = H_LOCAL - WIDTH_A
STAGES = 4


def dot_nn(a, b):
    return jnp.dot(a, b, preferred_element_type=F32)


def dot_nt(a, b):
    return lax.dot_general(a, b, (((1,), (1,)), ((), ())), preferred_element_type=F32)


def dot_tn(a, b):
    return lax.dot_general(a, b, (((0,), (0,)), ((), ())), preferred_element_type=F32)


def swiglu_back(gate, upper, hidden_grad):
    sig = jax.nn.sigmoid(gate)
    act = gate * sig
    hidden = (act * upper).astype(BF16)
    gate_delta = (hidden_grad * upper * sig * (1.0 + gate * (1.0 - sig))).astype(BF16)
    up_delta = (hidden_grad * act).astype(BF16)
    return hidden, gate_delta, up_delta


def exchange_kernel(
    act_in, grad_in, wg_in, wu_in, wd_in,
    tokens_out, delta_out, input_grad_out,
    wg, wu, wd, tok, part_a, part_b,
    send_a1, recv_a1, send_a2, recv_a2,
    send_b1, recv_b1, send_b2, recv_b2,
    delta_a, delta_b, igrad, core_recv, x_recv, z_recv,
    load_sem, gather_s, gather_r,
    a1_s, a1_r, a2_s, a2_r, b1_s, b1_r, b2_s, b2_r,
    ga1_s, ga1_r, ga2_s, ga2_r, gb1_s, gb1_r, gb2_s, gb2_r,
    core_s, core_r, x_s, x_r, z_s, z_r, out_sem,
):
    row = lax.axis_index("row")
    col = lax.axis_index("col")
    y = lax.rem(row, 4)
    zl = lax.div(row, 4)
    zh = lax.div(col, 8)
    x = lax.rem(lax.div(col, 2), 4)
    core = lax.rem(col, 2)

    def at_y(dist):
        return (zl * 4 + lax.rem(y + dist, 4), col)

    def at_x(dist):
        return (row, zh * 8 + lax.rem(x + dist, 4) * 2 + core)

    z_pair = ((1 - zl) * 4 + y, col)
    zh_pair = (row, (1 - zh) * 8 + x * 2 + core)
    sibling = (row, zh * 8 + x * 2 + 1 - core)
    partners = [at_y(1), at_y(2), at_y(3), z_pair, at_x(1), at_x(2), at_x(3), zh_pair, sibling]

    def remote(src, dst, send, recv, device):
        return pltpu.make_async_remote_copy(
            src_ref=src, dst_ref=dst, send_sem=send, recv_sem=recv,
            device_id=device, device_id_type=MESH,
        )

    own_row = core * 96 + zh * BLOCK
    loads = [
        pltpu.make_async_copy(act_in, tok.at[0, pl.ds(own_row, BLOCK)], load_sem.at[0]),
        pltpu.make_async_copy(grad_in, tok.at[1, pl.ds(own_row, BLOCK)], load_sem.at[1]),
        pltpu.make_async_copy(wg_in, wg, load_sem.at[2]),
        pltpu.make_async_copy(wu_in, wu, load_sem.at[3]),
        pltpu.make_async_copy(wd_in, wd, load_sem.at[4]),
    ]
    for load in loads:
        load.start()

    barrier = pltpu.get_barrier_semaphore()
    for device in partners:
        pl.semaphore_signal(barrier, inc=1, device_id=device, device_id_type=MESH)
    pl.semaphore_wait(barrier, len(partners))

    def blk(slot, core_, zh_):
        return tok.at[:, pl.ds(slot * SLOT + core_ * 96 + zh_ * BLOCK, BLOCK)]

    slot_dist = (0, 1, 3, 2)
    slot_at = (0, 2, 1, 3)

    def to_zh():
        return remote(blk(0, core, zh), blk(0, core, zh), gather_s.at[0], gather_r.at[0], zh_pair)

    def to_sibling(slot, which):
        zh_ = zh if which == 0 else 1 - zh
        sem = 1 + which if slot == 0 else 3 + 4 * (slot - 1) + 2 + which
        return remote(blk(slot, core, zh_), blk(slot, core, zh_), gather_s.at[sem], gather_r.at[sem], sibling)

    def to_x(slot, which):
        zh_ = zh if which == 0 else 1 - zh
        sem = 3 + 4 * (slot - 1) + which
        return remote(
            blk(0, core, zh_), blk(slot, core, zh_), gather_s.at[sem], gather_r.at[sem],
            at_x(slot_dist[slot_at[slot]]),
        )

    loads[0].wait()
    loads[1].wait()
    to_zh().start()
    to_sibling(0, 0).start()
    for slot in (1, 2, 3):
        to_x(slot, 0).start()
    to_zh().wait_recv()
    to_sibling(0, 1).start()
    for slot in (1, 2, 3):
        to_x(slot, 1).start()
    for which in (0, 1):
        to_sibling(0, which).wait_recv()
    for load in loads[2:]:
        load.wait()

    def slot_arrives(slot):
        for which in (0, 1):
            to_x(slot, which).wait_recv()
            to_sibling(slot, which).start()
        for which in (0, 1):
            to_sibling(slot, which).wait_recv()

    plane = pl.ds(64 * zl, 64)
    other_plane = pl.ds(64 * (1 - zl), 64)

    def copy_a1(c):
        return remote(send_a1.at[c], recv_a1.at[c], a1_s.at[c], a1_r.at[c], z_pair)

    def copy_a2(c, d):
        src = send_a2.at[c, :, pl.ds(OWN * lax.rem(y + d, 4), OWN)]
        return remote(src, recv_a2.at[c, d - 1], a2_s.at[c, d - 1], a2_r.at[c, d - 1], at_y(d))

    def copy_b1(c, d):
        src = send_b1.at[c, :, pl.ds(32 * lax.rem(y + d, 4), 32)]
        return remote(src, recv_b1.at[c, d - 1], b1_s.at[c, d - 1], b1_r.at[c, d - 1], at_y(d))

    def copy_b2(c):
        return remote(send_b2.at[c], recv_b2.at[c], b2_s.at[c], b2_r.at[c], z_pair)

    def gather_a1(c, d):
        src = delta_a.at[:, pl.ds(c * CHUNK + 64 * zl + OWN * y, OWN)]
        return remote(src, src, ga1_s.at[c, d - 1], ga1_r.at[c, d - 1], at_y(d))

    def gather_a2(c):
        src = delta_a.at[:, pl.ds(c * CHUNK + 64 * zl, 64)]
        return remote(src, src, ga2_s.at[c], ga2_r.at[c], z_pair)

    def gather_b1(c):
        src = delta_b.at[:, pl.ds(c * CHUNK + 32 * y + OWN * zl, OWN)]
        return remote(src, src, gb1_s.at[c], gb1_r.at[c], z_pair)

    def gather_b2(c, d):
        src = delta_b.at[:, pl.ds(c * CHUNK + 32 * y, 32)]
        return remote(src, src, gb2_s.at[c, d - 1], gb2_r.at[c, d - 1], at_y(d))

    def out_copies(c):
        rows = pl.ds(c * CHUNK, CHUNK)
        return (
            pltpu.make_async_copy(delta_a.at[:, rows], delta_out.at[:, rows, pl.ds(0, WIDTH_A)], out_sem.at[0, c]),
            pltpu.make_async_copy(delta_b.at[:, rows], delta_out.at[:, rows, pl.ds(WIDTH_A, WIDTH_B)], out_sem.at[1, c]),
        )

    tokens_copy = pltpu.make_async_copy(tok, tokens_out, load_sem.at[0])

    def stage0(c):
        p = lax.rem(c, 2)
        rows = pl.ds(c * CHUNK, CHUNK)
        act, grad = tok[0, rows, :], tok[1, rows, :]
        part_a[p, 0] = dot_nn(act, wg[:, :WIDTH_A])
        part_a[p, 1] = dot_nn(act, wu[:, :WIDTH_A])
        part_a[p, 2] = dot_nt(grad, wd[:WIDTH_A, :])
        for i in range(3):
            send_a1[c, i] = part_a[p, i, other_plane, :].astype(BF16)
        copy_a1(c).start()
        part_b[p, 0] = dot_nn(act, wg[:, WIDTH_A:])
        part_b[p, 1] = dot_nn(act, wu[:, WIDTH_A:])
        part_b[p, 2] = dot_nt(grad, wd[WIDTH_A:, :])
        for i in range(3):
            send_b1[c, i] = part_b[p, i].astype(BF16)
        for d in (2, 1, 3):
            copy_b1(c, d).start()

    def stage1(c):
        p = lax.rem(c, 2)
        copy_a1(c).wait_recv()
        for i in range(3):
            total = part_a[p, i, plane, :] + recv_a1[c, i].astype(F32)
            part_a[p, i, plane, :] = total
            send_a2[c, i] = total.astype(BF16)
        for d in (2, 1, 3):
            copy_a2(c, d).start()
        for d in (1, 2, 3):
            copy_b1(c, d).wait_recv()
        mine = pl.ds(32 * y, 32)
        for i in range(3):
            total = part_b[p, i, mine, :]
            for d in range(3):
                total = total + recv_b1[c, d, i].astype(F32)
            part_b[p, i, mine, :] = total
            send_b2[c, i] = part_b[p, i, pl.ds(32 * y + OWN * (1 - zl), OWN), :].astype(BF16)
        copy_b2(c).start()

    def stage2(c):
        p = lax.rem(c, 2)
        for d in (1, 2, 3):
            copy_a2(c, d).wait_recv()
        own = pl.ds(64 * zl + OWN * y, OWN)
        sums = []
        for i in range(3):
            total = part_a[p, i, own, :]
            for d in range(3):
                total = total + recv_a2[c, d, i].astype(F32)
            sums.append(total)
        for i, value in enumerate(swiglu_back(*sums)):
            delta_a[i, pl.ds(c * CHUNK + 64 * zl + OWN * y, OWN), :] = value
        for d in (2, 1, 3):
            gather_a1(c, d).start()
        copy_b2(c).wait_recv()
        own = pl.ds(32 * y + OWN * zl, OWN)
        sums = [part_b[p, i, own, :] + recv_b2[c, i].astype(F32) for i in range(3)]
        for i, value in enumerate(swiglu_back(*sums)):
            delta_b[i, pl.ds(c * CHUNK + 32 * y + OWN * zl, OWN), :] = value
        gather_b1(c).start()

    def recv_rows(ref, start, size, send, recv, device):
        view = ref.at[:, pl.ds(start, size)]
        return remote(view, view, send, recv, device)

    def stage3(c):
        for d in (1, 2, 3):
            start = c * CHUNK + 64 * zl + OWN * lax.rem(y + 4 - d, 4)
            recv_rows(delta_a, start, OWN, ga1_s.at[c, d - 1], ga1_r.at[c, d - 1], at_y(d)).wait_recv()
        gather_a2(c).start()
        start = c * CHUNK + 32 * y + OWN * (1 - zl)
        recv_rows(delta_b, start, OWN, gb1_s.at[c], gb1_r.at[c], z_pair).wait_recv()
        for d in (2, 1, 3):
            gather_b2(c, d).start()

    def stage4(c):
        recv_rows(delta_a, c * CHUNK + 64 * (1 - zl), 64, ga2_s.at[c], ga2_r.at[c], z_pair).wait_recv()
        for d in (1, 2, 3):
            start = c * CHUNK + 32 * lax.rem(y + 4 - d, 4)
            recv_rows(delta_b, start, 32, gb2_s.at[c, d - 1], gb2_r.at[c, d - 1], at_y(d)).wait_recv()
        for copy in out_copies(c):
            copy.start()
        rows = pl.ds(c * CHUNK, CHUNK)
        igrad[rows, :] = dot_nt(delta_a[1, rows, :], wg[:, :WIDTH_A])
        igrad[rows, :] += dot_nt(delta_b[1, rows, :], wg[:, WIDTH_A:])
        igrad[rows, :] += dot_nt(delta_a[2, rows, :], wu[:, :WIDTH_A])
        igrad[rows, :] += dot_nt(delta_b[2, rows, :], wu[:, WIDTH_A:])

    def core_rows(slot, core_):
        return pl.ds(slot * SLOT + core_ * 96, 96)

    def core_copy(slot):
        return remote(
            igrad.at[core_rows(slot, 1 - core)], core_recv.at[slot], core_s.at[slot], core_r.at[slot], sibling
        )

    def x_copy(slot):
        return remote(
            igrad.at[core_rows(slot, core)], x_recv.at[slot - 1], x_s.at[slot - 1], x_r.at[slot - 1],
            at_x(slot_dist[slot]),
        )

    def z_copy():
        return remote(
            igrad.at[pl.ds(core * 96 + (1 - zh) * BLOCK, BLOCK)], z_recv, z_s.at[0], z_r.at[0], zh_pair
        )

    def sum_core(slot):
        core_copy(slot).wait_recv()
        rows = core_rows(slot, core)
        igrad[rows, :] = igrad[rows, :] + core_recv[slot]
        if slot:
            x_copy(slot).start()

    last_chunk = (1, 2, 4, 5)

    @pl.loop(0, CHUNKS + STAGES)
    def _(t):
        @pl.when(t >= 4)
        def _():
            stage4(t - 4)

        for slot in range(4):
            @pl.when(t == last_chunk[slot] + 4)
            def _():
                core_copy(slot).start()

        @pl.when((t >= 3) & (t < CHUNKS + 3))
        def _():
            stage3(t - 3)

        @pl.when((t >= 2) & (t < CHUNKS + 2))
        def _():
            stage2(t - 2)

        @pl.when((t >= 1) & (t < CHUNKS + 1))
        def _():
            stage1(t - 1)

        for slot in (1, 2, 3):
            @pl.when(t == slot)
            def _():
                slot_arrives(slot)

        @pl.when(t < CHUNKS)
        def _():
            stage0(t)

        @pl.when(t == 3)
        def _():
            tokens_copy.start()

        for slot in range(3):
            @pl.when(t == last_chunk[slot] + 5)
            def _():
                sum_core(slot)

    sum_core(3)
    rows = core_rows(0, core)
    for slot in (1, 2, 3):
        x_copy(slot).wait_recv()
        igrad[rows, :] = igrad[rows, :] + x_recv[slot - 1]
    z_copy().start()
    z_copy().wait_recv()
    mine = pl.ds(own_row, BLOCK)
    input_grad_out[...] = (igrad[mine, :] + z_recv[...]).astype(BF16)

    to_zh().wait_send()
    for which in (0, 1):
        for slot in (1, 2, 3):
            to_x(slot, which).wait_send()
        for slot in range(4):
            to_sibling(slot, which).wait_send()

    @pl.loop(0, CHUNKS)
    def _(c):
        copy_a1(c).wait_send()
        copy_b2(c).wait_send()
        gather_a2(c).wait_send()
        gather_b1(c).wait_send()
        for d in (1, 2, 3):
            copy_a2(c, d).wait_send()
            copy_b1(c, d).wait_send()
            gather_a1(c, d).wait_send()
            gather_b2(c, d).wait_send()
        for copy in out_copies(c):
            copy.wait()

    for slot in range(4):
        core_copy(slot).wait_send()
    for slot in (1, 2, 3):
        x_copy(slot).wait_send()
    z_copy().wait_send()
    tokens_copy.wait()


def exchange(activations, out_grad, w_gate, w_up, w_down):
    dma = pltpu.SemaphoreType.DMA
    any_spec = pl.BlockSpec(memory_space=pl.ANY)
    n = CHUNKS
    return pl.pallas_call(
        exchange_kernel,
        out_shape=[
            jax.ShapeDtypeStruct((2, TOKENS, D_LOCAL), BF16),
            jax.ShapeDtypeStruct((3, TOKENS, H_LOCAL), BF16),
            jax.ShapeDtypeStruct((BLOCK, D_LOCAL), BF16),
        ],
        in_specs=[any_spec] * 5,
        out_specs=[any_spec, any_spec, pl.BlockSpec(memory_space=pltpu.VMEM)],
        scratch_shapes=[
            pltpu.VMEM((D_LOCAL, H_LOCAL), BF16),
            pltpu.VMEM((D_LOCAL, H_LOCAL), BF16),
            pltpu.VMEM((H_LOCAL, D_LOCAL), BF16),
            pltpu.VMEM((2, TOKENS, D_LOCAL), BF16),
            pltpu.VMEM((2, 3, CHUNK, WIDTH_A), F32),
            pltpu.VMEM((2, 3, CHUNK, WIDTH_B), F32),
            pltpu.VMEM((n, 3, 64, WIDTH_A), BF16),
            pltpu.VMEM((n, 3, 64, WIDTH_A), BF16),
            pltpu.VMEM((n, 3, 64, WIDTH_A), BF16),
            pltpu.VMEM((n, 3, 3, OWN, WIDTH_A), BF16),
            pltpu.VMEM((n, 3, CHUNK, WIDTH_B), BF16),
            pltpu.VMEM((n, 3, 3, 32, WIDTH_B), BF16),
            pltpu.VMEM((n, 3, OWN, WIDTH_B), BF16),
            pltpu.VMEM((n, 3, OWN, WIDTH_B), BF16),
            pltpu.VMEM((3, TOKENS, WIDTH_A), BF16),
            pltpu.VMEM((3, TOKENS, WIDTH_B), BF16),
            pltpu.VMEM((TOKENS, D_LOCAL), F32),
            pltpu.VMEM((4, 96, D_LOCAL), F32),
            pltpu.VMEM((3, 96, D_LOCAL), F32),
            pltpu.VMEM((BLOCK, D_LOCAL), F32),
            dma((5,)), dma((15,)), dma((15,)),
            dma((n,)), dma((n,)), dma((n, 3)), dma((n, 3)),
            dma((n, 3)), dma((n, 3)), dma((n,)), dma((n,)),
            dma((n, 3)), dma((n, 3)), dma((n,)), dma((n,)),
            dma((n,)), dma((n,)), dma((n, 3)), dma((n, 3)),
            dma((4,)), dma((4,)), dma((3,)), dma((3,)), dma((1,)), dma((1,)),
            dma((2, n)),
        ],
        compiler_params=pltpu.CompilerParams(
            collective_id=0, has_side_effects=True, vmem_limit_bytes=60 * 2**20
        ),
        cost_estimate=pl.CostEstimate(
            flops=10 * TOKENS * D_LOCAL * H_LOCAL, bytes_accessed=22 * 2**20, transcendentals=0
        ),
        name="exchange",
    )(activations, out_grad, w_gate, w_up, w_down)


def weights_kernel(
    tok_in, delta_in, gate_out, up_out, down_out,
    tok, delta, gate, up, down, in_sem, out_sem,
):
    loads = [
        pltpu.make_async_copy(tok_in.at[0], tok.at[0], in_sem.at[0]),
        pltpu.make_async_copy(delta_in.at[1], delta.at[1], in_sem.at[1]),
        pltpu.make_async_copy(delta_in.at[2], delta.at[2], in_sem.at[2]),
        pltpu.make_async_copy(delta_in.at[0], delta.at[0], in_sem.at[3]),
        pltpu.make_async_copy(tok_in.at[1], tok.at[1], in_sem.at[4]),
    ]
    for load in loads:
        load.start()
    stores = []

    def store(src, dst, start, size):
        copy = pltpu.make_async_copy(
            src.at[pl.ds(start, size)], dst.at[pl.ds(start, size)], out_sem.at[len(stores)]
        )
        copy.start()
        stores.append(copy)

    loads[0].wait()
    for load, i, buf, out in ((loads[1], 1, gate, gate_out), (loads[2], 2, up, up_out)):
        load.wait()
        for m in range(0, D_LOCAL, 256):
            buf[m : m + 256, :] = dot_tn(tok[0, :, m : m + 256], delta[i]).astype(BF16)
            store(buf, out, m, 256)
    loads[3].wait()
    loads[4].wait()
    for m in range(0, H_LOCAL, 256):
        size = min(256, H_LOCAL - m)
        down[m : m + size, :] = dot_tn(delta[0, :, m : m + size], tok[1]).astype(BF16)
        store(down, down_out, m, size)
    for copy in stores:
        copy.wait()


def weight_grads(tokens, deltas):
    any_spec = pl.BlockSpec(memory_space=pl.ANY)
    shapes = [(D_LOCAL, H_LOCAL), (D_LOCAL, H_LOCAL), (H_LOCAL, D_LOCAL)]
    return pl.pallas_call(
        weights_kernel,
        out_shape=[jax.ShapeDtypeStruct(s, BF16) for s in shapes],
        in_specs=[any_spec] * 2,
        out_specs=[any_spec] * 3,
        scratch_shapes=[
            pltpu.VMEM((2, TOKENS, D_LOCAL), BF16),
            pltpu.VMEM((3, TOKENS, H_LOCAL), BF16),
            *[pltpu.VMEM(s, BF16) for s in shapes],
            pltpu.SemaphoreType.DMA((5,)),
            pltpu.SemaphoreType.DMA((15,)),
        ],
        compiler_params=pltpu.CompilerParams(vmem_limit_bytes=56 * 2**20),
        cost_estimate=pl.CostEstimate(
            flops=6 * TOKENS * D_LOCAL * H_LOCAL, bytes_accessed=22 * 2**20, transcendentals=0
        ),
        name="weight_grads",
    )(tokens, deltas)


def per_device(activations, out_grad, w_gate, w_up, w_down):
    tokens, deltas, input_grad = exchange(activations, out_grad, w_gate, w_up, w_down)
    gate_grad, up_grad, down_grad = weight_grads(tokens, deltas)
    return input_grad, gate_grad, up_grad, down_grad


def solution(mesh):
    placed = (P("col", "row"), P("col", "row"), P("row", "col"), P("row", "col"), P("col", "row"))
    return jax.shard_map(
        per_device,
        mesh=mesh,
        in_specs=placed,
        out_specs=(P("col", "row"), P("row", "col"), P("row", "col"), P("col", "row")),
        check_vma=False,
    )
```

time: 528 us -> 188 us (0.36)
  the two profiles are of different devices: /device:TPU:0 before, /device:TPU:10 now
where the time goes in v1:
time: 188 us
  Pallas kernels  187 us (99%)
    pallas_call x1, Pallas kernels, exchange(): pl.pallas_call(exchange_kernel, out_shape=[jax.ShapeDtypeStruct((2, TOKEN...  175 us
    pallas_call x1, Pallas kernels, weight_grads(): pl.pallas_call(weights_kernel, out_shape=[jax.ShapeDtypeStruct(s, BF16) f...  12.1 us

profile of v1, /device:TPU:10, one launch (start us, length us, event | category | flops | bytes accessed | tf_op | source)
XLA Modules:
  0.0 187.9 jit_solution(14544725116598500200)
XLA Ops:
  0.6 174.5 %exchange.1 = (bf16[2,768,1024]{2,1,0:T(8,128)(2,1)}, bf16[3,768,1664]{2,1,0:T(8,128)(2,1)}, bf16[48,1024]{1,0:T(8,128)(2,1)}) custom-call(bf16[48,1024]{1,0:T(8,128)(2,1)} %act_in.1, bf16[48,1024]{1,0:T(8,128)(2,1)} %grad_in.1, bf16[1024,1664]{1,0:T(8,128)(2,1)} %wg_in.1, bf16[1024,1664]{1,0:T(8,128)(2,1)} %wu_in.1, bf16[1664,1024]{1,0:T(8,128)(2,1)} %wd_in.1), custom_call_target="tpu_custom_call" | custom-call | flops 13086228480 | bytes 23068672 | tf_op jit(solution)/shard_map/exchange/pallas_call | solution.py:386
  175.2 0.0 copy-start
  175.2 12.1 %weight_grads.1 = (bf16[1024,1664]{1,0:T(8,128)(2,1)}, bf16[1024,1664]{1,0:T(8,128)(2,1)}, bf16[1664,1024]{1,0:T(8,128)(2,1)}) custom-call(bf16[2,768,1024]{2,1,0:T(8,128)(2,1)} %get-tuple-element.11.tok_in, bf16[3,768,1664]{2,1,0:T(8,128)(2,1)} %get-tuple-element.12.delta_in), custom_call_target="tpu_custom_call" | custom-call | flops 7851737088 | bytes 23068672 | tf_op jit(solution)/shard_map/weight_grads/pallas_call | solution.py:475
  187.3 0.0 copy-done
  187.3 0.6 copy.10
Async XLA Ops:
  175.2 12.1 %copy-start = (bf16[48,1024]{1,0:T(8,128)(2,1)S(1)}, bf16[48,1024]{1,0:T(8,128)(2,1)}, u32[]{:S(2)}) copy-start(bf16[48,1024]{1,0:T(8,128)(2,1)} %get-tuple-element.20) | copy-start | bytes 294916

commit v2 on v0

v2 whole, which is shorter than its diff:
```python
import functools

import jax
import jax.numpy as jnp
from jax import lax
from jax.experimental import pallas as pl
from jax.experimental.pallas import tpu as pltpu
from jax.sharding import PartitionSpec as P

F32 = jnp.float32
BF16 = jnp.bfloat16
MESH = pl.DeviceIdType.MESH

CHUNKS = 6
CHUNK = 128
OWN = 16
SLOTS = 4
D_LOCAL = 1024
H_LOCAL = 1664
TOKENS = 768
BLOCK = 48
UNIT = 96
WIDTH_A = 640
HALF_A = 384
WIDTH_B = H_LOCAL - WIDTH_A


def dot_nn(a, b):
    return jnp.dot(a, b, preferred_element_type=F32)


def dot_nt(a, b):
    return lax.dot_general(a, b, (((1,), (1,)), ((), ())), preferred_element_type=F32)


def dot_tn(a, b):
    return lax.dot_general(a, b, (((0,), (0,)), ((), ())), preferred_element_type=F32)


def swiglu_back(gate, upper, hidden_grad):
    sig = jax.nn.sigmoid(gate)
    act = gate * sig
    hidden = (act * upper).astype(BF16)
    gate_delta = (hidden_grad * upper * sig * (1.0 + gate * (1.0 - sig))).astype(BF16)
    up_delta = (hidden_grad * act).astype(BF16)
    return hidden, gate_delta, up_delta


def exchange_kernel(
    act_in, grad_in, wg_in, wu_in, wd_in,
    tokens_out, delta_out, near_out, other_out, far_out,
    wg, wu, wd, tok, part_a, part_b,
    send_az, recv_az, send_ay, recv_af, recv_as, recv_ay,
    send_by, recv_bu, recv_by, send_bz, recv_bz,
    delta_a, delta_b, igrad, core_recv, x_recv,
    load_sem, zh_s, zh_r, sib_s, sib_r, tokx_s, tokx_r,
    az_s, az_r, bz_s, bz_r, gaz_s, gaz_r, gbz_s, gbz_r,
    ay_s, ay_r, by_s, by_r, gay_s, gay_r, gby_s, gby_r,
    core_s, core_r, x_s, x_r, out_sem,
):
    row = lax.axis_index("row")
    col = lax.axis_index("col")
    y = lax.rem(row, 4)
    zl = lax.div(row, 4)
    zh = lax.div(col, 8)
    x = lax.rem(lax.div(col, 2), 4)
    core = lax.rem(col, 2)
    y_next, y_prev, y_far = lax.rem(y + 1, 4), lax.rem(y + 3, 4), lax.rem(y + 2, 4)

    def at_x(dist):
        return (row, zh * 8 + lax.rem(x + dist, 4) * 2 + core)

    up_y = (zl * 4 + y_next, col)
    down_y = (zl * 4 + y_prev, col)
    z_pair = ((1 - zl) * 4 + y, col)
    zh_pair = (row, (1 - zh) * 8 + x * 2 + core)
    sibling = (row, zh * 8 + x * 2 + 1 - core)
    partners = [up_y, down_y, z_pair, at_x(1), at_x(2), at_x(3), zh_pair, sibling]

    def remote(src, dst, send, recv, device):
        return pltpu.make_async_remote_copy(
            src_ref=src, dst_ref=dst, send_sem=send, recv_sem=recv,
            device_id=device, device_id_type=MESH,
        )

    unit_dist = (0, 1, 3, 2, 1, 3, 2, 0)
    to_unit = {(0, 3): 1, (0, 1): 2, (0, 2): 3, (1, 3): 4, (1, 1): 5, (1, 2): 6}

    def blk(unit, core_):
        return tok.at[:, pl.ds(unit * UNIT + core_ * BLOCK, BLOCK)]

    def to_zh():
        return remote(blk(0, core), blk(7, core), zh_s.at[0], zh_r.at[0], zh_pair)

    def to_sibling(unit):
        return remote(blk(unit, core), blk(unit, core), sib_s.at[unit], sib_r.at[unit], sibling)

    def to_x(other, dist):
        unit = to_unit[other, dist]
        return remote(blk(7 * other, core), blk(unit, core), tokx_s.at[unit - 1], tokx_r.at[unit - 1], at_x(dist))

    def pass_on(unit):
        if unit == 7:
            to_zh().wait_recv()
        else:
            view = blk(unit, core)
            remote(view, view, tokx_s.at[unit - 1], tokx_r.at[unit - 1], at_x(unit_dist[unit])).wait_recv()
        to_sibling(unit).start()

    own = pl.ds(core * BLOCK, BLOCK)
    loads = [
        pltpu.make_async_copy(act_in, tok.at[0, own], load_sem.at[0]),
        pltpu.make_async_copy(grad_in, tok.at[1, own], load_sem.at[1]),
        pltpu.make_async_copy(wg_in, wg, load_sem.at[2]),
        pltpu.make_async_copy(wu_in, wu, load_sem.at[3]),
        pltpu.make_async_copy(wd_in, wd, load_sem.at[4]),
    ]
    for load in loads:
        load.start()

    barrier = pltpu.get_barrier_semaphore()
    for device in partners:
        pl.semaphore_signal(barrier, inc=1, device_id=device, device_id_type=MESH)
    pl.semaphore_wait(barrier, len(partners))

    loads[0].wait()
    loads[1].wait()
    to_x(0, 3).start()
    to_x(0, 1).start()
    to_sibling(0).start()
    to_zh().start()
    to_x(0, 2).start()
    pass_on(1)
    for load in loads[2:]:
        load.wait()
    to_sibling(0).wait_recv()
    to_sibling(1).wait_recv()

    def rows_a(c, y_):
        return pl.ds(c * CHUNK + 64 * zl + OWN * y_, OWN)

    def rows_b(c, y_, first, size):
        return pl.ds(c * CHUNK + 32 * y_ + first, size)

    first_a, second_a = pl.ds(0, HALF_A), pl.ds(HALF_A, WIDTH_A - HALF_A)

    def send_az_copy(c):
        return remote(send_az.at[c], recv_az.at[c], az_s.at[c], az_r.at[c], z_pair)

    def send_bz_copy(c):
        return remote(send_bz.at[c], recv_bz.at[c], bz_s.at[c], bz_r.at[c], z_pair)

    def ay(c, k):
        def src(y_, cols):
            return send_ay.at[c, :, pl.ds(OWN * y_, OWN), cols]

        sem = (ay_s.at[c, k], ay_r.at[c, k])
        if k == 0:
            return remote(src(y_far, first_a), recv_af.at[c], *sem, up_y)
        if k == 1:
            return remote(src(y_far, second_a), recv_as.at[c], *sem, down_y)
        if k == 2:
            return remote(src(y_next, second_a), recv_ay.at[c, 0, :, :, second_a], *sem, up_y)
        if k == 3:
            return remote(src(y_prev, first_a), recv_ay.at[c, 1, :, :, first_a], *sem, down_y)
        if k == 4:
            return remote(src(y_next, first_a), recv_ay.at[c, 0, :, :, first_a], *sem, up_y)
        return remote(src(y_prev, second_a), recv_ay.at[c, 1, :, :, second_a], *sem, down_y)

    def by(c, k):
        def src(y_, half):
            return send_by.at[c, :, pl.ds(32 * y_ + OWN * half, OWN)]

        def dst(side, half):
            return recv_by.at[c, side, :, pl.ds(OWN * half, OWN)]

        sem = (by_s.at[c, k], by_r.at[c, k])
        if k == 0:
            return remote(src(y_far, 0), recv_bu.at[c, 0], *sem, up_y)
        if k == 1:
            return remote(src(y_far, 1), recv_bu.at[c, 1], *sem, down_y)
        if k == 2:
            return remote(src(y_next, 1), dst(0, 1), *sem, up_y)
        if k == 3:
            return remote(src(y_prev, 0), dst(1, 0), *sem, down_y)
        if k == 4:
            return remote(src(y_next, 0), dst(0, 0), *sem, up_y)
        return remote(src(y_prev, 1), dst(1, 1), *sem, down_y)

    def same(view, send, recv, device):
        return remote(view, view, send, recv, device)

    def gather_az(c, zl_):
        view = delta_a.at[:, pl.ds(c * CHUNK + 64 * zl_, 64)]
        return same(view, gaz_s.at[c], gaz_r.at[c], z_pair)

    def gather_bz(c, zl_):
        return same(delta_b.at[:, rows_b(c, y, OWN * zl_, OWN)], gbz_s.at[c], gbz_r.at[c], z_pair)

    def gather_ay(c, k, y_):
        sem = (gay_s.at[c, k], gay_r.at[c, k])
        rows = rows_a(c, y_)
        view = (delta_a.at[:, rows], delta_a.at[:, rows],
                delta_a.at[:, rows, second_a], delta_a.at[:, rows, first_a])[k]
        return same(view, *sem, down_y if k % 2 else up_y)

    def gather_by(c, k, y_):
        sem = (gby_s.at[c, k], gby_r.at[c, k])
        rows = (rows_b(c, y_, 0, 32), rows_b(c, y_, 0, 32), rows_b(c, y_, OWN, OWN), rows_b(c, y_, 0, OWN))[k]
        return same(delta_b.at[:, rows], *sem, down_y if k % 2 else up_y)

    def out_copies(c):
        rows = pl.ds(c * CHUNK, CHUNK)
        return (
            pltpu.make_async_copy(delta_a.at[:, rows], delta_out.at[:, rows, pl.ds(0, WIDTH_A)], out_sem.at[0, c]),
            pltpu.make_async_copy(delta_b.at[:, rows], delta_out.at[:, rows, pl.ds(WIDTH_A, WIDTH_B)], out_sem.at[1, c]),
        )

    tokens_copy = pltpu.make_async_copy(tok, tokens_out, load_sem.at[0])

    def partial_a(c):
        p = lax.rem(c, SLOTS)
        rows = pl.ds(c * CHUNK, CHUNK)
        act, grad = tok[0, rows, :], tok[1, rows, :]
        part_a[p, 0] = dot_nn(act, wg[:, :WIDTH_A])
        part_a[p, 1] = dot_nn(act, wu[:, :WIDTH_A])
        part_a[p, 2] = dot_nt(grad, wd[:WIDTH_A, :])
        for i in range(3):
            send_az[c, i] = part_a[p, i, pl.ds(64 * (1 - zl), 64), :].astype(BF16)
        send_az_copy(c).start()

    def partial_b(c):
        p = lax.rem(c, SLOTS)
        rows = pl.ds(c * CHUNK, CHUNK)
        act, grad = tok[0, rows, :], tok[1, rows, :]
        part_b[p, 0] = dot_nn(act, wg[:, WIDTH_A:])
        part_b[p, 1] = dot_nn(act, wu[:, WIDTH_A:])
        part_b[p, 2] = dot_nt(grad, wd[WIDTH_A:, :])
        for i in range(3):
            send_by[c, i] = part_b[p, i].astype(BF16)
        for k in range(4):
            by(c, k).start()

    def plane_a(c):
        p = lax.rem(c, SLOTS)
        send_az_copy(c).wait_recv()
        plane = pl.ds(64 * zl, 64)
        for i in range(3):
            total = part_a[p, i, plane, :] + recv_az[c, i].astype(F32)
            part_a[p, i, plane, :] = total
            send_ay[c, i] = total.astype(BF16)
        for k in range(4):
            ay(c, k).start()

    def ring_a(c):
        p = lax.rem(c, SLOTS)
        ay(c, 0).wait_recv()
        for i in range(3):
            total = part_a[p, i, pl.ds(64 * zl + OWN * y_next, OWN), :HALF_A] + recv_af[c, i].astype(F32)
            send_ay[c, i, pl.ds(OWN * y_next, OWN), :HALF_A] = total.astype(BF16)
        ay(c, 4).start()
        ay(c, 1).wait_recv()
        for i in range(3):
            total = part_a[p, i, pl.ds(64 * zl + OWN * y_prev, OWN), HALF_A:] + recv_as[c, i].astype(F32)
            send_ay[c, i, pl.ds(OWN * y_prev, OWN), HALF_A:] = total.astype(BF16)
        ay(c, 5).start()

    def ring_b(c):
        p = lax.rem(c, SLOTS)
        for side, y_ in ((0, y_next), (1, y_prev)):
            by(c, side).wait_recv()
            mine = pl.ds(32 * y_ + OWN * side, OWN)
            for i in range(3):
                total = part_b[p, i, mine, :] + recv_bu[c, side, i].astype(F32)
                send_by[c, i, mine, :] = total.astype(BF16)
            by(c, 4 + side).start()

    def own_a(c):
        p = lax.rem(c, SLOTS)
        for k in range(2, 6):
            ay(c, k).wait_recv()
        mine = pl.ds(64 * zl + OWN * y, OWN)
        sums = [
            part_a[p, i, mine, :] + recv_ay[c, 0, i].astype(F32) + recv_ay[c, 1, i].astype(F32)
            for i in range(3)
        ]
        for i, value in enumerate(swiglu_back(*sums)):
            delta_a[i, rows_a(c, y), :] = value
        for k in range(2):
            gather_ay(c, k, y).start()

    def own_b(c):
        p = lax.rem(c, SLOTS)
        for k in range(2, 6):
            by(c, k).wait_recv()
        for half in range(2):
            mine = pl.ds(32 * y + OWN * half, OWN)
            for i in range(3):
                total = part_b[p, i, mine, :]
                for side in range(2):
                    total = total + recv_by[c, side, i, pl.ds(OWN * half, OWN), :].astype(F32)
                part_b[p, i, mine, :] = total
        for i in range(3):
            send_bz[c, i] = part_b[p, i, pl.ds(32 * y + OWN * (1 - zl), OWN), :].astype(BF16)
        send_bz_copy(c).start()

    def point_b(c):
        p = lax.rem(c, SLOTS)
        send_bz_copy(c).wait_recv()
        mine = pl.ds(32 * y + OWN * zl, OWN)
        sums = [part_b[p, i, mine, :] + recv_bz[c, i].astype(F32) for i in range(3)]
        for i, value in enumerate(swiglu_back(*sums)):
            delta_b[i, rows_b(c, y, OWN * zl, OWN), :] = value
        gather_bz(c, zl).start()

    def forward_a(c):
        gather_ay(c, 0, y_prev).wait_recv()
        gather_ay(c, 2, y_prev).start()
        gather_ay(c, 1, y_next).wait_recv()
        gather_ay(c, 3, y_next).start()

    def quarter_b(c):
        gather_bz(c, 1 - zl).wait_recv()
        for k in range(2):
            gather_by(c, k, y).start()

    def swap_a(c):
        for k in (2, 3):
            gather_ay(c, k, y_far).wait_recv()
        gather_az(c, zl).start()

    def forward_b(c):
        gather_by(c, 0, y_prev).wait_recv()
        gather_by(c, 2, y_prev).start()
        gather_by(c, 1, y_next).wait_recv()
        gather_by(c, 3, y_next).start()

    def input_grad_part(c):
        rows = pl.ds(c * CHUNK, CHUNK)
        gather_az(c, 1 - zl).wait_recv()
        igrad[rows, :] = dot_nt(delta_a[1, rows, :], wg[:, :WIDTH_A])
        igrad[rows, :] += dot_nt(delta_a[2, rows, :], wu[:, :WIDTH_A])
        for k in (2, 3):
            gather_by(c, k, y_far).wait_recv()
        for copy in out_copies(c):
            copy.start()
        igrad[rows, :] += dot_nt(delta_b[1, rows, :], wg[:, WIDTH_A:])
        igrad[rows, :] += dot_nt(delta_b[2, rows, :], wu[:, WIDTH_A:])

    def unit_rows(unit, core_):
        return pl.ds(unit * UNIT + core_ * BLOCK, BLOCK)

    def core_copy(unit):
        return remote(
            igrad.at[unit_rows(unit, 1 - core)], core_recv.at[unit], core_s.at[unit], core_r.at[unit], sibling
        )

    def x_copy(unit):
        return remote(
            igrad.at[unit_rows(unit, core)], x_recv.at[unit - 1], x_s.at[unit - 1], x_r.at[unit - 1],
            at_x(unit_dist[unit]),
        )

    def sum_core(unit):
        core_copy(unit).wait_recv()
        rows = unit_rows(unit, core)
        igrad[rows, :] = igrad[rows, :] + core_recv[unit]
        if 1 <= unit <= 5:
            x_copy(unit).start()

    stages = (
        (6, input_grad_part), (5, swap_a), (5, forward_b), (4, forward_a), (4, quarter_b),
        (3, own_a), (3, point_b), (2, ring_a), (2, own_b), (1, plane_a), (1, ring_b),
        (0, partial_a), (0, partial_b),
    )
    units_done = ((0,), (1,), (2, 3), (4,), (5,), (6, 7))
    units_wait = ((), (2,), (3,), (4, 5), (6,), (7,))
    units_pass = ((2,), (7, 3), (4, 5), (6,), (), ())

    @pl.loop(0, CHUNKS + 6)
    def _(t):
        for delay, stage in stages:
            if delay == 0 and stage is partial_a:
                for c in range(1, CHUNKS):
                    @pl.when(t == c)
                    def _():
                        for unit in units_wait[c]:
                            to_sibling(unit).wait_recv()

            @pl.when((t >= delay) & (t < CHUNKS + delay))
            def _():
                stage(t - delay)

            if delay == 6:
                for c in range(CHUNKS):
                    @pl.when(t == c + 6)
                    def _():
                        for unit in units_done[c]:
                            core_copy(unit).start()

        for c in range(4):
            @pl.when(t == c)
            def _():
                for unit in units_pass[c]:
                    pass_on(unit)
                    if unit == 7:
                        for dist in (3, 1, 2):
                            to_x(1, dist).start()

        @pl.when(t == CHUNKS - 1)
        def _():
            tokens_copy.start()

        for c in range(CHUNKS - 1):
            @pl.when(t == c + 6)
            def _():
                for unit in units_done[c]:
                    sum_core(unit)

    near = igrad[unit_rows(0, core), :]
    for unit in (1, 2, 3):
        x_copy(unit).wait_recv()
        near = near + x_recv[unit - 1]
    near_out[...] = near
    for unit in (6, 7):
        sum_core(unit)
    far_out[...] = igrad[unit_rows(6, core), :]
    other = igrad[unit_rows(7, core), :]
    for unit in (4, 5):
        x_copy(unit).wait_recv()
        other = other + x_recv[unit - 1]
    other_out[...] = other

    to_zh().wait_send()
    for other_, dist in to_unit:
        to_x(other_, dist).wait_send()
    for unit in range(8):
        to_sibling(unit).wait_send()
        core_copy(unit).wait_send()
    for unit in range(1, 6):
        x_copy(unit).wait_send()

    @pl.loop(0, CHUNKS)
    def _(c):
        send_az_copy(c).wait_send()
        send_bz_copy(c).wait_send()
        gather_az(c, zl).wait_send()
        gather_bz(c, zl).wait_send()
        for k in range(6):
            ay(c, k).wait_send()
            by(c, k).wait_send()
        for k in range(4):
            gather_ay(c, k, y).wait_send()
            gather_by(c, k, y).wait_send()
        for copy in out_copies(c):
            copy.wait()

    tokens_copy.wait()


def exchange(activations, out_grad, w_gate, w_up, w_down):
    dma = pltpu.SemaphoreType.DMA
    any_spec = pl.BlockSpec(memory_space=pl.ANY)
    vmem_spec = pl.BlockSpec(memory_space=pltpu.VMEM)
    n = CHUNKS
    return pl.pallas_call(
        exchange_kernel,
        out_shape=[
            jax.ShapeDtypeStruct((2, TOKENS, D_LOCAL), BF16),
            jax.ShapeDtypeStruct((3, TOKENS, H_LOCAL), BF16),
            *[jax.ShapeDtypeStruct((BLOCK, D_LOCAL), F32)] * 3,
        ],
        in_specs=[any_spec] * 5,
        out_specs=[any_spec] * 2 + [vmem_spec] * 3,
        scratch_shapes=[
            pltpu.VMEM((D_LOCAL, H_LOCAL), BF16),
            pltpu.VMEM((D_LOCAL, H_LOCAL), BF16),
            pltpu.VMEM((H_LOCAL, D_LOCAL), BF16),
            pltpu.VMEM((2, TOKENS, D_LOCAL), BF16),
            pltpu.VMEM((SLOTS, 3, CHUNK, WIDTH_A), F32),
            pltpu.VMEM((SLOTS, 3, CHUNK, WIDTH_B), F32),
            pltpu.VMEM((n, 3, 64, WIDTH_A), BF16),
            pltpu.VMEM((n, 3, 64, WIDTH_A), BF16),
            pltpu.VMEM((n, 3, 64, WIDTH_A), BF16),
            pltpu.VMEM((n, 3, OWN, HALF_A), BF16),
            pltpu.VMEM((n, 3, OWN, WIDTH_A - HALF_A), BF16),
            pltpu.VMEM((n, 2, 3, OWN, WIDTH_A), BF16),
            pltpu.VMEM((n, 3, CHUNK, WIDTH_B), BF16),
            pltpu.VMEM((n, 2, 3, OWN, WIDTH_B), BF16),
            pltpu.VMEM((n, 2, 3, 32, WIDTH_B), BF16),
            pltpu.VMEM((n, 3, OWN, WIDTH_B), BF16),
            pltpu.VMEM((n, 3, OWN, WIDTH_B), BF16),
            pltpu.VMEM((3, TOKENS, WIDTH_A), BF16),
            pltpu.VMEM((3, TOKENS, WIDTH_B), BF16),
            pltpu.VMEM((TOKENS, D_LOCAL), F32),
            pltpu.VMEM((8, BLOCK, D_LOCAL), F32),
            pltpu.VMEM((5, BLOCK, D_LOCAL), F32),
            dma((5,)), dma((1,)), dma((1,)), dma((8,)), dma((8,)), dma((6,)), dma((6,)),
            *[dma((n,))] * 8,
            dma((n, 6)), dma((n, 6)), dma((n, 6)), dma((n, 6)),
            dma((n, 4)), dma((n, 4)), dma((n, 4)), dma((n, 4)),
            dma((8,)), dma((8,)), dma((5,)), dma((5,)),
            dma((2, n)),
        ],
        compiler_params=pltpu.CompilerParams(
            collective_id=0, has_side_effects=True, vmem_limit_bytes=60 * 2**20
        ),
        cost_estimate=pl.CostEstimate(
            flops=10 * TOKENS * D_LOCAL * H_LOCAL, bytes_accessed=22 * 2**20, transcendentals=0
        ),
        name="exchange",
    )(activations, out_grad, w_gate, w_up, w_down)


def weights_kernel(
    tok_in, delta_in, gate_out, up_out, down_out,
    tok, delta, gate, up, down, in_sem, out_sem,
):
    loads = [
        pltpu.make_async_copy(tok_in.at[0], tok.at[0], in_sem.at[0]),
        pltpu.make_async_copy(delta_in.at[1], delta.at[1], in_sem.at[1]),
        pltpu.make_async_copy(delta_in.at[2], delta.at[2], in_sem.at[2]),
        pltpu.make_async_copy(delta_in.at[0], delta.at[0], in_sem.at[3]),
        pltpu.make_async_copy(tok_in.at[1], tok.at[1], in_sem.at[4]),
    ]
    for load in loads:
        load.start()
    stores = []

    def store(src, dst, start, size):
        copy = pltpu.make_async_copy(
            src.at[pl.ds(start, size)], dst.at[pl.ds(start, size)], out_sem.at[len(stores)]
        )
        copy.start()
        stores.append(copy)

    loads[0].wait()
    for load, i, buf, out in ((loads[1], 1, gate, gate_out), (loads[2], 2, up, up_out)):
        load.wait()
        for m in range(0, D_LOCAL, 256):
            buf[m : m + 256, :] = dot_tn(tok[0, :, m : m + 256], delta[i]).astype(BF16)
            store(buf, out, m, 256)
    loads[3].wait()
    loads[4].wait()
    for m in range(0, H_LOCAL, 256):
        size = min(256, H_LOCAL - m)
        down[m : m + size, :] = dot_tn(delta[0, :, m : m + size], tok[1]).astype(BF16)
        store(down, down_out, m, size)
    for copy in stores:
        copy.wait()


def weight_grads(tokens, deltas):
    any_spec = pl.BlockSpec(memory_space=pl.ANY)
    shapes = [(D_LOCAL, H_LOCAL), (D_LOCAL, H_LOCAL), (H_LOCAL, D_LOCAL)]
    return pl.pallas_call(
        weights_kernel,
        out_shape=[jax.ShapeDtypeStruct(s, BF16) for s in shapes],
        in_specs=[any_spec] * 2,
        out_specs=[any_spec] * 3,
        scratch_shapes=[
            pltpu.VMEM((2, TOKENS, D_LOCAL), BF16),
            pltpu.VMEM((3, TOKENS, H_LOCAL), BF16),
            *[pltpu.VMEM(s, BF16) for s in shapes],
            pltpu.SemaphoreType.DMA((5,)),
            pltpu.SemaphoreType.DMA((15,)),
        ],
        compiler_params=pltpu.CompilerParams(vmem_limit_bytes=56 * 2**20),
        cost_estimate=pl.CostEstimate(
            flops=6 * TOKENS * D_LOCAL * H_LOCAL, bytes_accessed=22 * 2**20, transcendentals=0
        ),
        name="weight_grads",
    )(tokens, deltas)


def per_device(activations, out_grad, w_gate, w_up, w_down):
    tokens, deltas, near, other, far = exchange(activations, out_grad, w_gate, w_up, w_down)

    def moved(c, dist):
        return (1 - c // 8) * 8 + ((c // 2 + dist) % 4) * 2 + c % 2

    other = lax.ppermute(other, "col", [(c, moved(c, 0)) for c in range(16)])
    far = lax.ppermute(far, "col", [(c, moved(c, 2)) for c in range(16)])
    gate_grad, up_grad, down_grad = weight_grads(tokens, deltas)
    input_grad = (near + other + far).astype(BF16)
    return input_grad, gate_grad, up_grad, down_grad


def solution(mesh):
    placed = (P("col", "row"), P("col", "row"), P("row", "col"), P("row", "col"), P("col", "row"))
    return jax.shard_map(
        per_device,
        mesh=mesh,
        in_specs=placed,
        out_specs=(P("col", "row"), P("row", "col"), P("row", "col"), P("col", "row")),
        check_vma=False,
    )
```

time: 528 us -> 149 us (0.28)
  waiting for transfers between devices: 451 us -> 0.01 us
  Pallas kernels: 0 us -> 141 us
  matrix products: 47.1 us -> 0 us
  between operations: 13.8 us -> 0.67 us
  local copies, waits for them, and re-layouts: 7.78 us -> 0.01 us
  other arithmetic: 8.22 us -> 0.67 us
  starting transfers between devices: 0.34 us -> 5.77 us
    psum x1 -> x0, waiting for transfers between devices: 315 us -> none  [per_device(): lax.psum((gate_part, upper_part, hgrad_part), 'row')]
    pallas_call x0 -> x2, Pallas kernels: none -> 141 us  [the longest x1 129 us: exchange(): pl.pallas_call(exchange_kernel, out_shape=[jax.ShapeDtypeStruct((2, TOKEN...]
    all_gather x2 -> x0, waiting for transfers between devices: 87.4 us -> none  [the longest x1 51.1 us: per_device(): lax.all_gather(activations, 'col', axis=0, tiled=True)]
    reduce_scatter x1 -> x0, waiting for transfers between devices: 47.6 us -> none  [per_device(): lax.psum_scatter(contract_last(gate_delta, w_gate) + contract_last(up_del...]
    dot_general x8 -> x0, matrix products: 47.1 us -> none  [the longest x3 19.9 us: contract_first(): lax.dot_general(left, right, (((0,), (0,)), ((), ())), preferred_element_...]
    unnamed x16 -> x2, local copies, waits for them, and re-layouts: 7.78 us -> 0.01 us
    convert_element_type x2 -> x1, other arithmetic: 8.22 us -> 0.67 us  [per_device(): input_grad = (near + other + far).astype(BF16)]
    ppermute x0 -> x2, starting transfers between devices: none -> 5.77 us  [the longest x1 3.04 us: per_device(): far = lax.ppermute(far, 'col', [(c, moved(c, 2)) for c in range(16)])]
  transfers between devices with their start and end apart: 4 -> 2, of which waited for: 4 -> 0; matrix products, arithmetic and copies ran while one was open for 7% -> 0% of each run, Pallas kernels for 0% -> 8%
where the time goes in v2:
time: 149 us; the launch traced here: 148 us
  Pallas kernels  141 us (95%)
  starting transfers between devices  5.77 us (4%)
    pallas_call x1, Pallas kernels, exchange(): pl.pallas_call(exchange_kernel, out_shape=[jax.ShapeDtypeStruct((2, TOKEN...  129 us
    pallas_call x1, Pallas kernels, weight_grads(): pl.pallas_call(weights_kernel, out_shape=[jax.ShapeDtypeStruct(s, BF16) f...  12.1 us
    ppermute x1, starting transfers between devices, per_device(): far = lax.ppermute(far, 'col', [(c, moved(c, 2)) for c in range(16)])  3.04 us
  transfers between devices with their start and end apart: 2, of which 0 were waited for; matrix products, arithmetic and copies ran while one was open for 0% of the time, Pallas kernels for 8%

profile of v2, /device:TPU:0, one launch (start us, length us, event | category | flops | bytes accessed | tf_op | source)
XLA Modules:
  0.0 148.2 jit_solution(12405595830575211619)
XLA Ops:
  0.6 128.9 %exchange.1 = (bf16[2,768,1024]{2,1,0:T(8,128)(2,1)}, bf16[3,768,1664]{2,1,0:T(8,128)(2,1)}, f32[48,1024]{1,0:T(8,128)}, f32[48,1024]{1,0:T(8,128)}, f32[48,1024]{1,0:T(8,128)}) custom-call(bf16[48,1024]{1,0:T(8,128)(2,1)} %act_in.1, bf16[48,1024]{1,0:T(8,128)(2,1)} %grad_in.1, bf16[1024,1664]{1,0:T(8,128)(2,1)} %wg_in.1, bf16[1024,1664]{1,0:T(8,128)(2,1)} %wu_in.1, ...), custom_call_target="tpu_custom_call" | custom-call | flops 13086228480 | bytes 23068672 | tf_op jit(solution)/shard_map/exchange/pallas_call | solution.py:466
  129.6 2.7 %collective-permute-start = (f32[48,1024]{1,0:T(8,128)}, f32[48,1024]{1,0:T(8,128)S(1)}, u32[]{:S(2)}, u32[]{:S(2)}) collective-permute-start(f32[48,1024]{1,0:T(8,128)} %get-tuple-element.13), channel_id=1, source_target_pairs={{0,8},{1,9},{2,10},{3,11},{4,12},{5,13},{6,14},{7,15},{8,0},{9,1},... | collective-permute-start | bytes 589832 | tf_op jit(solution)/shard_map/ppermute | solution.py:582
  132.3 3.0 %collective-permute-start.1 = (f32[48,1024]{1,0:T(8,128)}, f32[48,1024]{1,0:T(8,128)S(1)}, u32[]{:S(2)}, u32[]{:S(2)}) collective-permute-start(f32[48,1024]{1,0:T(8,128)} %get-tuple-element.14), channel_id=1, source_target_pairs={{0,12},{1,13},{2,14},{3,15},{4,8},{5,9},{6,10},{7,11},{8,4},{9,5},... | collective-permute-start | bytes 589832 | tf_op jit(solution)/shard_map/ppermute | solution.py:583
  135.3 0.0 copy-start
  135.3 12.1 %weight_grads.1 = (bf16[1024,1664]{1,0:T(8,128)(2,1)}, bf16[1024,1664]{1,0:T(8,128)(2,1)}, bf16[1664,1024]{1,0:T(8,128)(2,1)}) custom-call(bf16[2,768,1024]{2,1,0:T(8,128)(2,1)} %get-tuple-element.15.tok_in, bf16[3,768,1664]{2,1,0:T(8,128)(2,1)} %get-tuple-element.16.delta_in), custom_call_target="tpu_custom_call" | custom-call | flops 7851737088 | bytes 23068672 | tf_op jit(solution)/shard_map/weight_grads/pallas_call | solution.py:556
  147.5 0.0 collective-permute-done
  147.5 0.0 collective-permute-done.1
  147.5 0.0 copy-done
  147.5 0.7 add_convert_fusion
Async XLA Ops:
  129.6 17.9 %collective-permute-start = (f32[48,1024]{1,0:T(8,128)}, f32[48,1024]{1,0:T(8,128)S(1)}, u32[]{:S(2)}, u32[]{:S(2)}) collective-permute-start(f32[48,1024]{1,0:T(8,128)} %get-tuple-element.13), channel_id=1, source_target_pairs={{0,8},{1,9},{2,10},{3,11},{4,12},{5,13},{6,14},{7,15},{8,0},{9,1},... | collective-permute-start | bytes 589832 | tf_op jit(solution)/shard_map/ppermute | solution.py:582
  132.3 15.2 %collective-permute-start.1 = (f32[48,1024]{1,0:T(8,128)}, f32[48,1024]{1,0:T(8,128)S(1)}, u32[]{:S(2)}, u32[]{:S(2)}) collective-permute-start(f32[48,1024]{1,0:T(8,128)} %get-tuple-element.14), channel_id=1, source_target_pairs={{0,12},{1,13},{2,14},{3,15},{4,8},{5,9},{6,10},{7,11},{8,4},{9,5},... | collective-permute-start | bytes 589832 | tf_op jit(solution)/shard_map/ppermute | solution.py:583
  135.3 12.1 %copy-start = (f32[48,1024]{1,0:T(8,128)S(1)}, f32[48,1024]{1,0:T(8,128)}, u32[]{:S(2)}) copy-start(f32[48,1024]{1,0:T(8,128)} %get-tuple-element.12) | copy-start | bytes 589828

commit v3 on v2

--- a/solution.py
+++ b/solution.py
@@ -19,10 +19,14 @@
 H_LOCAL = 1664
 TOKENS = 768
 BLOCK = 48
-UNIT = 96
-WIDTH_A = 640
+WIDTH_A = 768
 HALF_A = 384
 WIDTH_B = H_LOCAL - WIDTH_A
+LEAD = 32
+BLOCK_ORDER = (
+    (0, 0), (0, 1), (1, 0), (2, 0), (3, 0), (1, 1), (2, 1), (3, 1),
+    (4, 0), (4, 1), (5, 0), (5, 1), (6, 0), (6, 1), (7, 0), (7, 1),
+)
 
 
 def dot_nn(a, b):
@@ -48,7 +52,7 @@
 
 def exchange_kernel(
     act_in, grad_in, wg_in, wu_in, wd_in,
-    tokens_out, delta_out, near_out, other_out, far_out,
+    tokens_out, delta_out, near_out, other_out,
     wg, wu, wd, tok, part_a, part_b,
     send_az, recv_az, send_ay, recv_af, recv_as, recv_ay,
     send_by, recv_bu, recv_by, send_bz, recv_bz,
@@ -83,37 +87,44 @@
             device_id=device, device_id_type=MESH,
         )
 
-    unit_dist = (0, 1, 3, 2, 1, 3, 2, 0)
-    to_unit = {(0, 3): 1, (0, 1): 2, (0, 2): 3, (1, 3): 4, (1, 1): 5, (1, 2): 6}
-
-    def blk(unit, core_):
-        return tok.at[:, pl.ds(unit * UNIT + core_ * BLOCK, BLOCK)]
+    unit_dist = (0, 1, 3, 2, 2, 1, 3, 0)
+    to_unit = {(0, 3): 1, (0, 1): 2, (0, 2): 3, (1, 2): 4, (1, 3): 5, (1, 1): 6}
+
+    def at(unit, other_core):
+        return BLOCK * BLOCK_ORDER.index((unit, other_core))
+
+    def blk(unit, other_core):
+        return tok.at[:, pl.ds(at(unit, other_core), BLOCK)]
 
     def to_zh():
-        return remote(blk(0, core), blk(7, core), zh_s.at[0], zh_r.at[0], zh_pair)
+        return remote(blk(0, 0), blk(7, 0), zh_s.at[0], zh_r.at[0], zh_pair)
 
     def to_sibling(unit):
-        return remote(blk(unit, core), blk(unit, core), sib_s.at[unit], sib_r.at[unit], sibling)
+        return remote(blk(unit, 0), blk(unit, 1), sib_s.at[unit], sib_r.at[unit], sibling)
 
     def to_x(other, dist):
         unit = to_unit[other, dist]
-        return remote(blk(7 * other, core), blk(unit, core), tokx_s.at[unit - 1], tokx_r.at[unit - 1], at_x(dist))
+        return remote(blk(7 * other, 0), blk(unit, 0), tokx_s.at[unit - 1], tokx_r.at[unit - 1], at_x(dist))
 
     def pass_on(unit):
         if unit == 7:
             to_zh().wait_recv()
+            for dist in (2, 3, 1):
+                to_x(1, dist).start()
         else:
-            view = blk(unit, core)
+            view = blk(unit, 0)
             remote(view, view, tokx_s.at[unit - 1], tokx_r.at[unit - 1], at_x(unit_dist[unit])).wait_recv()
         to_sibling(unit).start()
 
-    own = pl.ds(core * BLOCK, BLOCK)
+    again = pl.ds(TOKENS, LEAD)
     loads = [
-        pltpu.make_async_copy(act_in, tok.at[0, own], load_sem.at[0]),
-        pltpu.make_async_copy(grad_in, tok.at[1, own], load_sem.at[1]),
-        pltpu.make_async_copy(wg_in, wg, load_sem.at[2]),
-        pltpu.make_async_copy(wu_in, wu, load_sem.at[3]),
-        pltpu.make_async_copy(wd_in, wd, load_sem.at[4]),
+        pltpu.make_async_copy(act_in, tok.at[0, pl.ds(0, BLOCK)], load_sem.at[0]),
+        pltpu.make_async_copy(grad_in, tok.at[1, pl.ds(0, BLOCK)], load_sem.at[1]),
+        pltpu.make_async_copy(act_in.at[pl.ds(0, LEAD)], tok.at[0, again], load_sem.at[2]),
+        pltpu.make_async_copy(grad_in.at[pl.ds(0, LEAD)], tok.at[1, again], load_sem.at[3]),
+        pltpu.make_async_copy(wg_in, wg, load_sem.at[4]),
+        pltpu.make_async_copy(wu_in, wu, load_sem.at[5]),
+        pltpu.make_async_copy(wd_in, wd, load_sem.at[6]),
     ]
     for load in loads:
         load.start()
@@ -130,11 +141,11 @@
     to_sibling(0).start()
     to_zh().start()
     to_x(0, 2).start()
-    pass_on(1)
     for load in loads[2:]:
         load.wait()
     to_sibling(0).wait_recv()
-    to_sibling(1).wait_recv()
+    pass_on(1)
+    pass_on(2)
 
     def rows_a(c, y_):
         return pl.ds(c * CHUNK + 64 * zl + OWN * y_, OWN)
@@ -216,11 +227,11 @@
             pltpu.make_async_copy(delta_b.at[:, rows], delta_out.at[:, rows, pl.ds(WIDTH_A, WIDTH_B)], out_sem.at[1, c]),
         )
 
-    tokens_copy = pltpu.make_async_copy(tok, tokens_out, load_sem.at[0])
+    tokens_copy = pltpu.make_async_copy(tok.at[:, pl.ds(LEAD, TOKENS)], tokens_out, load_sem.at[0])
 
     def partial_a(c):
         p = lax.rem(c, SLOTS)
-        rows = pl.ds(c * CHUNK, CHUNK)
+        rows = pl.ds(LEAD + c * CHUNK, CHUNK)
         act, grad = tok[0, rows, :], tok[1, rows, :]
         part_a[p, 0] = dot_nn(act, wg[:, :WIDTH_A])
         part_a[p, 1] = dot_nn(act, wu[:, :WIDTH_A])
@@ -231,7 +242,7 @@
 
     def partial_b(c):
         p = lax.rem(c, SLOTS)
-        rows = pl.ds(c * CHUNK, CHUNK)
+        rows = pl.ds(LEAD + c * CHUNK, CHUNK)
         act, grad = tok[0, rows, :], tok[1, rows, :]
         part_b[p, 0] = dot_nn(act, wg[:, WIDTH_A:])
         part_b[p, 1] = dot_nn(act, wu[:, WIDTH_A:])
@@ -335,52 +346,50 @@
         gather_by(c, 1, y_next).wait_recv()
         gather_by(c, 3, y_next).start()
 
-    def input_grad_part(c):
-        rows = pl.ds(c * CHUNK, CHUNK)
+    def input_grad_a(c):
+        rows, out = pl.ds(c * CHUNK, CHUNK), pl.ds(LEAD + c * CHUNK, CHUNK)
         gather_az(c, 1 - zl).wait_recv()
-        igrad[rows, :] = dot_nt(delta_a[1, rows, :], wg[:, :WIDTH_A])
-        igrad[rows, :] += dot_nt(delta_a[2, rows, :], wu[:, :WIDTH_A])
+        igrad[out, :] = dot_nt(delta_a[1, rows, :], wg[:, :WIDTH_A])
+        igrad[out, :] += dot_nt(delta_a[2, rows, :], wu[:, :WIDTH_A])
+
+    def input_grad_b(c):
+        rows, out = pl.ds(c * CHUNK, CHUNK), pl.ds(LEAD + c * CHUNK, CHUNK)
         for k in (2, 3):
             gather_by(c, k, y_far).wait_recv()
         for copy in out_copies(c):
             copy.start()
-        igrad[rows, :] += dot_nt(delta_b[1, rows, :], wg[:, WIDTH_A:])
-        igrad[rows, :] += dot_nt(delta_b[2, rows, :], wu[:, WIDTH_A:])
-
-    def unit_rows(unit, core_):
-        return pl.ds(unit * UNIT + core_ * BLOCK, BLOCK)
+        igrad[out, :] += dot_nt(delta_b[1, rows, :], wg[:, WIDTH_A:])
+        igrad[out, :] += dot_nt(delta_b[2, rows, :], wu[:, WIDTH_A:])
 
     def core_copy(unit):
-        return remote(
-            igrad.at[unit_rows(unit, 1 - core)], core_recv.at[unit], core_s.at[unit], core_r.at[unit], sibling
-        )
+        src = igrad.at[pl.ds(at(unit, 1), BLOCK)]
+        return remote(src, core_recv.at[unit], core_s.at[unit], core_r.at[unit], sibling)
 
     def x_copy(unit):
-        return remote(
-            igrad.at[unit_rows(unit, core)], x_recv.at[unit - 1], x_s.at[unit - 1], x_r.at[unit - 1],
-            at_x(unit_dist[unit]),
-        )
+        src = igrad.at[pl.ds(at(unit, 0), BLOCK)]
+        return remote(src, x_recv.at[unit - 1], x_s.at[unit - 1], x_r.at[unit - 1], at_x(unit_dist[unit]))
 
     def sum_core(unit):
         core_copy(unit).wait_recv()
-        rows = unit_rows(unit, core)
+        rows = pl.ds(at(unit, 0), BLOCK)
         igrad[rows, :] = igrad[rows, :] + core_recv[unit]
-        if 1 <= unit <= 5:
-            x_copy(unit).start()
+        x_copy(unit).start()
 
     stages = (
-        (6, input_grad_part), (5, swap_a), (5, forward_b), (4, forward_a), (4, quarter_b),
-        (3, own_a), (3, point_b), (2, ring_a), (2, own_b), (1, plane_a), (1, ring_b),
-        (0, partial_a), (0, partial_b),
+        (0, partial_a), (5, swap_a), (0, partial_b), (4, forward_a), (1, ring_b), (1, plane_a), (2, own_b),
+        (3, point_b), (3, own_a), (2, ring_a), (4, quarter_b), (5, forward_b), (6, input_grad_a), (6, input_grad_b),
     )
-    units_done = ((0,), (1,), (2, 3), (4,), (5,), (6, 7))
-    units_wait = ((), (2,), (3,), (4, 5), (6,), (7,))
-    units_pass = ((2,), (7, 3), (4, 5), (6,), (), ())
-
-    @pl.loop(0, CHUNKS + 6)
+    units_done = ((0,), (1,), (2, 3), (4,), (5, 6), (7,))
+    units_wait = ((), (1,), (2, 3), (4, 5), (6,), (7,))
+    units_pass = ((3, 7), (4, 5), (6,))
+
+    first = [stage for delay, stage in stages if delay == 0][0]
+    last = max(delay for delay, _ in stages)
+
+    @pl.loop(0, CHUNKS + last)
     def _(t):
         for delay, stage in stages:
-            if delay == 0 and stage is partial_a:
+            if stage is first:
                 for c in range(1, CHUNKS):
                     @pl.when(t == c)
                     def _():
@@ -391,42 +400,40 @@
             def _():
                 stage(t - delay)
 
-            if delay == 6:
+            if stage is input_grad_b:
                 for c in range(CHUNKS):
-                    @pl.when(t == c + 6)
+                    @pl.when(t == c + last)
                     def _():
                         for unit in units_done[c]:
                             core_copy(unit).start()
 
-        for c in range(4):
+        for c, units in enumerate(units_pass):
             @pl.when(t == c)
             def _():
-                for unit in units_pass[c]:
+                for unit in units:
                     pass_on(unit)
-                    if unit == 7:
-                        for dist in (3, 1, 2):
-                            to_x(1, dist).start()
 
         @pl.when(t == CHUNKS - 1)
         def _():
             tokens_copy.start()
 
         for c in range(CHUNKS - 1):
-            @pl.when(t == c + 6)
+            @pl.when(t == c + last)
             def _():
                 for unit in units_done[c]:
-                    sum_core(unit)
-
-    near = igrad[unit_rows(0, core), :]
+                    if unit:
+                        sum_core(unit)
+
+    core_copy(0).wait_recv()
+    near = igrad[pl.ds(at(0, 0) + LEAD, BLOCK - LEAD), :], igrad[again, :]
+    near = jnp.concatenate([near[1], near[0]], axis=0) + core_recv[0]
     for unit in (1, 2, 3):
         x_copy(unit).wait_recv()
         near = near + x_recv[unit - 1]
     near_out[...] = near
-    for unit in (6, 7):
-        sum_core(unit)
-    far_out[...] = igrad[unit_rows(6, core), :]
-    other = igrad[unit_rows(7, core), :]
-    for unit in (4, 5):
+    core_copy(7).wait_recv()
+    other = igrad[pl.ds(at(7, 0), BLOCK), :] + core_recv[7]
+    for unit in (4, 5, 6):
         x_copy(unit).wait_recv()
         other = other + x_recv[unit - 1]
     other_out[...] = other
@@ -437,7 +444,7 @@
     for unit in range(8):
         to_sibling(unit).wait_send()
         core_copy(unit).wait_send()
-    for unit in range(1, 6):
+    for unit in range(1, 7):
         x_copy(unit).wait_send()
 
     @pl.loop(0, CHUNKS)
@@ -468,15 +475,15 @@
         out_shape=[
             jax.ShapeDtypeStruct((2, TOKENS, D_LOCAL), BF16),
             jax.ShapeDtypeStruct((3, TOKENS, H_LOCAL), BF16),
-            *[jax.ShapeDtypeStruct((BLOCK, D_LOCAL), F32)] * 3,
+            *[jax.ShapeDtypeStruct((BLOCK, D_LOCAL), F32)] * 2,
         ],
         in_specs=[any_spec] * 5,
-        out_specs=[any_spec] * 2 + [vmem_spec] * 3,
+        out_specs=[any_spec] * 2 + [vmem_spec] * 2,
         scratch_shapes=[
             pltpu.VMEM((D_LOCAL, H_LOCAL), BF16),
             pltpu.VMEM((D_LOCAL, H_LOCAL), BF16),
             pltpu.VMEM((H_LOCAL, D_LOCAL), BF16),
-            pltpu.VMEM((2, TOKENS, D_LOCAL), BF16),
+            pltpu.VMEM((2, TOKENS + LEAD, D_LOCAL), BF16),
             pltpu.VMEM((SLOTS, 3, CHUNK, WIDTH_A), F32),
             pltpu.VMEM((SLOTS, 3, CHUNK, WIDTH_B), F32),
             pltpu.VMEM((n, 3, 64, WIDTH_A), BF16),
@@ -492,14 +499,14 @@
             pltpu.VMEM((n, 3, OWN, WIDTH_B), BF16),
             pltpu.VMEM((3, TOKENS, WIDTH_A), BF16),
             pltpu.VMEM((3, TOKENS, WIDTH_B), BF16),
-            pltpu.VMEM((TOKENS, D_LOCAL), F32),
+            pltpu.VMEM((TOKENS + LEAD, D_LOCAL), F32),
             pltpu.VMEM((8, BLOCK, D_LOCAL), F32),
-            pltpu.VMEM((5, BLOCK, D_LOCAL), F32),
-            dma((5,)), dma((1,)), dma((1,)), dma((8,)), dma((8,)), dma((6,)), dma((6,)),
+            pltpu.VMEM((6, BLOCK, D_LOCAL), F32),
+            dma((7,)), dma((1,)), dma((1,)), dma((8,)), dma((8,)), dma((6,)), dma((6,)),
             *[dma((n,))] * 8,
             dma((n, 6)), dma((n, 6)), dma((n, 6)), dma((n, 6)),
             dma((n, 4)), dma((n, 4)), dma((n, 4)), dma((n, 4)),
-            dma((8,)), dma((8,)), dma((5,)), dma((5,)),
+            dma((8,)), dma((8,)), dma((6,)), dma((6,)),
             dma((2, n)),
         ],
         compiler_params=pltpu.CompilerParams(
@@ -574,16 +581,10 @@
 
 
 def per_device(activations, out_grad, w_gate, w_up, w_down):
-    tokens, deltas, near, other, far = exchange(activations, out_grad, w_gate, w_up, w_down)
-
-    def moved(c, dist):
-        return (1 - c // 8) * 8 + ((c // 2 + dist) % 4) * 2 + c % 2
-
-    other = lax.ppermute(other, "col", [(c, moved(c, 0)) for c in range(16)])
-    far = lax.ppermute(far, "col", [(c, moved(c, 2)) for c in range(16)])
+    tokens, deltas, near, other = exchange(activations, out_grad, w_gate, w_up, w_down)
+    other = lax.ppermute(other, "col", [(c, (c + 8) % 16) for c in range(16)])
     gate_grad, up_grad, down_grad = weight_grads(tokens, deltas)
-    input_grad = (near + other + far).astype(BF16)
-    return input_grad, gate_grad, up_grad, down_grad
+    return (near + other).astype(BF16), gate_grad, up_grad, down_grad
 
 
 def solution(mesh):

time: 149 us -> 144 us (0.966)
  starting transfers between devices: 5.77 us -> 1.58 us
    ppermute x2 -> x1, starting transfers between devices: 5.77 us -> 1.58 us  [per_device(): other = lax.ppermute(other, 'col', [(c, (c + 8) % 16) for c in range(16)])]
  transfers between devices with their start and end apart: 2 -> 1, of which waited for: 0 -> 0; matrix products, arithmetic and copies ran while one was open for 0% -> 0% of each run, Pallas kernels for 8% -> 8%
where the time goes in v3:
time: 144 us; the launch traced here: 142 us
  Pallas kernels  140 us (97%)
  starting transfers between devices  1.58 us (1%)
    pallas_call x1, Pallas kernels, exchange(): pl.pallas_call(exchange_kernel, out_shape=[jax.ShapeDtypeStruct((2, TOKEN...  127 us
    pallas_call x1, Pallas kernels, weight_grads(): pl.pallas_call(weights_kernel, out_shape=[jax.ShapeDtypeStruct(s, BF16) f...  12.1 us
  transfers between devices with their start and end apart: 1, of which 0 were waited for; matrix products, arithmetic and copies ran while one was open for 0% of the time, Pallas kernels for 8%

profile of v3, /device:TPU:0, one launch (start us, length us, event | category | flops | bytes accessed | tf_op | source)
XLA Modules:
  0.0 142.5 jit_solution(12419475182149318036)
XLA Ops:
  0.6 127.5 %exchange.1 = (bf16[2,768,1024]{2,1,0:T(8,128)(2,1)}, bf16[3,768,1664]{2,1,0:T(8,128)(2,1)}, f32[48,1024]{1,0:T(8,128)}, f32[48,1024]{1,0:T(8,128)}) custom-call(bf16[48,1024]{1,0:T(8,128)(2,1)} %act_in.1, bf16[48,1024]{1,0:T(8,128)(2,1)} %grad_in.1, bf16[1024,1664]{1,0:T(8,128)(2,1)} %wg_in.1, bf16[1024,1664]{1,0:T(8,128)(2,1)} %wu_in.1, ...), custom_call_target="tpu_custom_call" | custom-call | flops 13086228480 | bytes 23068672 | tf_op jit(solution)/shard_map/exchange/pallas_call | solution.py:473
  128.1 1.6 %collective-permute-start = (f32[48,1024]{1,0:T(8,128)}, f32[48,1024]{1,0:T(8,128)S(1)}, u32[]{:S(2)}, u32[]{:S(2)}) collective-permute-start(f32[48,1024]{1,0:T(8,128)} %get-tuple-element.12), channel_id=1, source_target_pairs={{0,8},{1,9},{2,10},{3,11},{4,12},{5,13},{6,14},{7,15},{8,0},{9,1},... | collective-permute-start | bytes 589832 | tf_op jit(solution)/shard_map/ppermute | solution.py:585
  129.7 0.0 copy-start
  129.7 12.1 %weight_grads.1 = (bf16[1024,1664]{1,0:T(8,128)(2,1)}, bf16[1024,1664]{1,0:T(8,128)(2,1)}, bf16[1664,1024]{1,0:T(8,128)(2,1)}) custom-call(bf16[2,768,1024]{2,1,0:T(8,128)(2,1)} %get-tuple-element.13.tok_in, bf16[3,768,1664]{2,1,0:T(8,128)(2,1)} %get-tuple-element.14.delta_in), custom_call_target="tpu_custom_call" | custom-call | flops 7851737088 | bytes 23068672 | tf_op jit(solution)/shard_map/weight_grads/pallas_call | solution.py:563
  141.8 0.0 collective-permute-done
  141.8 0.0 copy-done
  141.8 0.7 add_convert_fusion
Async XLA Ops:
  128.1 13.7 %collective-permute-start = (f32[48,1024]{1,0:T(8,128)}, f32[48,1024]{1,0:T(8,128)S(1)}, u32[]{:S(2)}, u32[]{:S(2)}) collective-permute-start(f32[48,1024]{1,0:T(8,128)} %get-tuple-element.12), channel_id=1, source_target_pairs={{0,8},{1,9},{2,10},{3,11},{4,12},{5,13},{6,14},{7,15},{8,0},{9,1},... | collective-permute-start | bytes 589832 | tf_op jit(solution)/shard_map/ppermute | solution.py:585
  129.7 12.1 %copy-start = (f32[48,1024]{1,0:T(8,128)S(1)}, f32[48,1024]{1,0:T(8,128)}, u32[]{:S(2)}) copy-start(f32[48,1024]{1,0:T(8,128)} %get-tuple-element.11) | copy-start | bytes 589828

commit v4 on v3

--- a/solution.py
+++ b/solution.py
@@ -93,28 +93,28 @@
     def at(unit, other_core):
         return BLOCK * BLOCK_ORDER.index((unit, other_core))
 
-    def blk(unit, other_core):
-        return tok.at[:, pl.ds(at(unit, other_core), BLOCK)]
-
-    def to_zh():
-        return remote(blk(0, 0), blk(7, 0), zh_s.at[0], zh_r.at[0], zh_pair)
-
-    def to_sibling(unit):
-        return remote(blk(unit, 0), blk(unit, 1), sib_s.at[unit], sib_r.at[unit], sibling)
-
-    def to_x(other, dist):
+    def blk(i, unit, other_core):
+        return tok.at[i, pl.ds(at(unit, other_core), BLOCK)]
+
+    def to_zh(i):
+        return remote(blk(i, 0, 0), blk(i, 7, 0), zh_s.at[i], zh_r.at[i], zh_pair)
+
+    def to_sibling(i, unit):
+        return remote(blk(i, unit, 0), blk(i, unit, 1), sib_s.at[i, unit], sib_r.at[i, unit], sibling)
+
+    def to_x(i, other, dist):
         unit = to_unit[other, dist]
-        return remote(blk(7 * other, 0), blk(unit, 0), tokx_s.at[unit - 1], tokx_r.at[unit - 1], at_x(dist))
-
-    def pass_on(unit):
+        return remote(blk(i, 7 * other, 0), blk(i, unit, 0), tokx_s.at[i, unit - 1], tokx_r.at[i, unit - 1], at_x(dist))
+
+    def pass_on(i, unit):
         if unit == 7:
-            to_zh().wait_recv()
+            to_zh(i).wait_recv()
             for dist in (2, 3, 1):
-                to_x(1, dist).start()
+                to_x(i, 1, dist).start()
         else:
-            view = blk(unit, 0)
-            remote(view, view, tokx_s.at[unit - 1], tokx_r.at[unit - 1], at_x(unit_dist[unit])).wait_recv()
-        to_sibling(unit).start()
+            view = blk(i, unit, 0)
+            remote(view, view, tokx_s.at[i, unit - 1], tokx_r.at[i, unit - 1], at_x(unit_dist[unit])).wait_recv()
+        to_sibling(i, unit).start()
 
     again = pl.ds(TOKENS, LEAD)
     loads = [
@@ -126,26 +126,31 @@
         pltpu.make_async_copy(wu_in, wu, load_sem.at[5]),
         pltpu.make_async_copy(wd_in, wd, load_sem.at[6]),
     ]
-    for load in loads:
-        load.start()
-
     barrier = pltpu.get_barrier_semaphore()
     for device in partners:
         pl.semaphore_signal(barrier, inc=1, device_id=device, device_id_type=MESH)
+    for load in loads:
+        load.start()
     pl.semaphore_wait(barrier, len(partners))
 
     loads[0].wait()
     loads[1].wait()
-    to_x(0, 3).start()
-    to_x(0, 1).start()
-    to_sibling(0).start()
-    to_zh().start()
-    to_x(0, 2).start()
-    for load in loads[2:]:
+    for i in range(2):
+        to_x(i, 0, 3).start()
+        to_x(i, 0, 1).start()
+        to_sibling(i, 0).start()
+    for i in range(2):
+        to_zh(i).start()
+        to_x(i, 0, 2).start()
+
+    def first_tokens(i):
+        to_sibling(i, 0).wait_recv()
+        pass_on(i, 1)
+        pass_on(i, 2)
+
+    for load in loads[2:6]:
         load.wait()
-    to_sibling(0).wait_recv()
-    pass_on(1)
-    pass_on(2)
+    first_tokens(0)
 
     def rows_a(c, y_):
         return pl.ds(c * CHUNK + 64 * zl + OWN * y_, OWN)
@@ -155,8 +160,8 @@
 
     first_a, second_a = pl.ds(0, HALF_A), pl.ds(HALF_A, WIDTH_A - HALF_A)
 
-    def send_az_copy(c):
-        return remote(send_az.at[c], recv_az.at[c], az_s.at[c], az_r.at[c], z_pair)
+    def send_az_copy(c, i):
+        return remote(send_az.at[c, i], recv_az.at[c, i], az_s.at[c, i], az_r.at[c, i], z_pair)
 
     def send_bz_copy(c):
         return remote(send_bz.at[c], recv_bz.at[c], bz_s.at[c], bz_r.at[c], z_pair)
@@ -201,9 +206,10 @@
     def same(view, send, recv, device):
         return remote(view, view, send, recv, device)
 
-    def gather_az(c, zl_):
-        view = delta_a.at[:, pl.ds(c * CHUNK + 64 * zl_, 64)]
-        return same(view, gaz_s.at[c], gaz_r.at[c], z_pair)
+    def gather_az(c, k, zl_):
+        y_ = (y, y_prev, y_next, y_far)[k]
+        view = delta_a.at[:, pl.ds(c * CHUNK + 64 * zl_ + OWN * y_, OWN)]
+        return same(view, gaz_s.at[c, k], gaz_r.at[c, k], z_pair)
 
     def gather_bz(c, zl_):
         return same(delta_b.at[:, rows_b(c, y, OWN * zl_, OWN)], gbz_s.at[c], gbz_r.at[c], z_pair)
@@ -232,21 +238,32 @@
     def partial_a(c):
         p = lax.rem(c, SLOTS)
         rows = pl.ds(LEAD + c * CHUNK, CHUNK)
-        act, grad = tok[0, rows, :], tok[1, rows, :]
+
+        def send(i):
+            send_az[c, i] = part_a[p, i, pl.ds(64 * (1 - zl), 64), :].astype(BF16)
+            send_az_copy(c, i).start()
+
+        act = tok[0, rows, :]
         part_a[p, 0] = dot_nn(act, wg[:, :WIDTH_A])
+        send(0)
         part_a[p, 1] = dot_nn(act, wu[:, :WIDTH_A])
-        part_a[p, 2] = dot_nt(grad, wd[:WIDTH_A, :])
-        for i in range(3):
-            send_az[c, i] = part_a[p, i, pl.ds(64 * (1 - zl), 64), :].astype(BF16)
-        send_az_copy(c).start()
+        send(1)
+
+        @pl.when(c == 0)
+        def _():
+            loads[6].wait()
+            first_tokens(1)
+
+        part_a[p, 2] = dot_nt(tok[1, rows, :], wd[:WIDTH_A, :])
+        send(2)
 
     def partial_b(c):
         p = lax.rem(c, SLOTS)
         rows = pl.ds(LEAD + c * CHUNK, CHUNK)
-        act, grad = tok[0, rows, :], tok[1, rows, :]
+        act = tok[0, rows, :]
         part_b[p, 0] = dot_nn(act, wg[:, WIDTH_A:])
         part_b[p, 1] = dot_nn(act, wu[:, WIDTH_A:])
-        part_b[p, 2] = dot_nt(grad, wd[WIDTH_A:, :])
+        part_b[p, 2] = dot_nt(tok[1, rows, :], wd[WIDTH_A:, :])
         for i in range(3):
             send_by[c, i] = part_b[p, i].astype(BF16)
         for k in range(4):
@@ -254,9 +271,9 @@
 
     def plane_a(c):
         p = lax.rem(c, SLOTS)
-        send_az_copy(c).wait_recv()
         plane = pl.ds(64 * zl, 64)
         for i in range(3):
+            send_az_copy(c, i).wait_recv()
             total = part_a[p, i, plane, :] + recv_az[c, i].astype(F32)
             part_a[p, i, plane, :] = total
             send_ay[c, i] = total.astype(BF16)
@@ -299,6 +316,7 @@
             delta_a[i, rows_a(c, y), :] = value
         for k in range(2):
             gather_ay(c, k, y).start()
+        gather_az(c, 0, zl).start()
 
     def own_b(c):
         p = lax.rem(c, SLOTS)
@@ -327,8 +345,10 @@
     def forward_a(c):
         gather_ay(c, 0, y_prev).wait_recv()
         gather_ay(c, 2, y_prev).start()
+        gather_az(c, 1, zl).start()
         gather_ay(c, 1, y_next).wait_recv()
         gather_ay(c, 3, y_next).start()
+        gather_az(c, 2, zl).start()
 
     def quarter_b(c):
         gather_bz(c, 1 - zl).wait_recv()
@@ -338,7 +358,7 @@
     def swap_a(c):
         for k in (2, 3):
             gather_ay(c, k, y_far).wait_recv()
-        gather_az(c, zl).start()
+        gather_az(c, 3, zl).start()
 
     def forward_b(c):
         gather_by(c, 0, y_prev).wait_recv()
@@ -348,7 +368,8 @@
 
     def input_grad_a(c):
         rows, out = pl.ds(c * CHUNK, CHUNK), pl.ds(LEAD + c * CHUNK, CHUNK)
-        gather_az(c, 1 - zl).wait_recv()
+        for k in range(4):
+            gather_az(c, k, 1 - zl).wait_recv()
         igrad[out, :] = dot_nt(delta_a[1, rows, :], wg[:, :WIDTH_A])
         igrad[out, :] += dot_nt(delta_a[2, rows, :], wu[:, :WIDTH_A])
 
@@ -376,8 +397,8 @@
         x_copy(unit).start()
 
     stages = (
-        (0, partial_a), (5, swap_a), (0, partial_b), (4, forward_a), (1, ring_b), (1, plane_a), (2, own_b),
-        (3, point_b), (3, own_a), (2, ring_a), (4, quarter_b), (5, forward_b), (6, input_grad_a), (6, input_grad_b),
+        (6, input_grad_a), (6, input_grad_b), (5, swap_a), (5, forward_b), (4, forward_a), (4, quarter_b),
+        (3, own_a), (3, point_b), (2, ring_a), (2, own_b), (1, plane_a), (1, ring_b), (0, partial_a), (0, partial_b),
     )
     units_done = ((0,), (1,), (2, 3), (4,), (5, 6), (7,))
     units_wait = ((), (1,), (2, 3), (4, 5), (6,), (7,))
@@ -394,7 +415,16 @@
                     @pl.when(t == c)
                     def _():
                         for unit in units_wait[c]:
-                            to_sibling(unit).wait_recv()
+                            for i in range(2):
+                                to_sibling(i, unit).wait_recv()
+
+            if stage is input_grad_a:
+                for c in range(CHUNKS - 1):
+                    @pl.when(t == c + last + 1)
+                    def _():
+                        for unit in units_done[c]:
+                            if unit:
+                                sum_core(unit)
 
             @pl.when((t >= delay) & (t < CHUNKS + delay))
             def _():
@@ -411,18 +441,12 @@
             @pl.when(t == c)
             def _():
                 for unit in units:
-                    pass_on(unit)
+                    for i in range(2):
+                        pass_on(i, unit)
 
         @pl.when(t == CHUNKS - 1)
         def _():
             tokens_copy.start()
-
-        for c in range(CHUNKS - 1):
-            @pl.when(t == c + last)
-            def _():
-                for unit in units_done[c]:
-                    if unit:
-                        sum_core(unit)
 
     core_copy(0).wait_recv()
     near = igrad[pl.ds(at(0, 0) + LEAD, BLOCK - LEAD), :], igrad[again, :]
@@ -438,20 +462,24 @@
         other = other + x_recv[unit - 1]
     other_out[...] = other
 
-    to_zh().wait_send()
-    for other_, dist in to_unit:
-        to_x(other_, dist).wait_send()
+    for i in range(2):
+        to_zh(i).wait_send()
+        for other_, dist in to_unit:
+            to_x(i, other_, dist).wait_send()
+        for unit in range(8):
+            to_sibling(i, unit).wait_send()
     for unit in range(8):
-        to_sibling(unit).wait_send()
         core_copy(unit).wait_send()
     for unit in range(1, 7):
         x_copy(unit).wait_send()
 
     @pl.loop(0, CHUNKS)
     def _(c):
-        send_az_copy(c).wait_send()
+        for i in range(3):
+            send_az_copy(c, i).wait_send()
         send_bz_copy(c).wait_send()
-        gather_az(c, zl).wait_send()
+        for k in range(4):
+            gather_az(c, k, zl).wait_send()
         gather_bz(c, zl).wait_send()
         for k in range(6):
             ay(c, k).wait_send()
@@ -502,8 +530,8 @@
             pltpu.VMEM((TOKENS + LEAD, D_LOCAL), F32),
             pltpu.VMEM((8, BLOCK, D_LOCAL), F32),
             pltpu.VMEM((6, BLOCK, D_LOCAL), F32),
-            dma((7,)), dma((1,)), dma((1,)), dma((8,)), dma((8,)), dma((6,)), dma((6,)),
-            *[dma((n,))] * 8,
+            dma((7,)), dma((2,)), dma((2,)), dma((2, 8)), dma((2, 8)), dma((2, 6)), dma((2, 6)),
+            dma((n, 3)), dma((n, 3)), dma((n,)), dma((n,)), dma((n, 4)), dma((n, 4)), dma((n,)), dma((n,)),
             dma((n, 6)), dma((n, 6)), dma((n, 6)), dma((n, 6)),
             dma((n, 4)), dma((n, 4)), dma((n, 4)), dma((n, 4)),
             dma((8,)), dma((8,)), dma((6,)), dma((6,)),

time: 144 us -> 142 us (0.986); the launches traced: 142 us -> 142 us
  Pallas kernels: 140 us -> 137 us
  starting transfers between devices: 1.58 us -> 3.32 us
    pallas_call x1, Pallas kernels: 127 us -> 125 us  [exchange(): pl.pallas_call(exchange_kernel, out_shape=[jax.ShapeDtypeStruct((2, TOKEN...]
    ppermute x1, starting transfers between devices: 1.58 us -> 3.32 us  [per_device(): other = lax.ppermute(other, 'col', [(c, (c + 8) % 16) for c in range(16)])]
where the time goes in v4:
time: 142 us
  Pallas kernels  137 us (96%)
  starting transfers between devices  3.32 us (2%)
    pallas_call x1, Pallas kernels, exchange(): pl.pallas_call(exchange_kernel, out_shape=[jax.ShapeDtypeStruct((2, TOKEN...  125 us
    pallas_call x1, Pallas kernels, weight_grads(): pl.pallas_call(weights_kernel, out_shape=[jax.ShapeDtypeStruct(s, BF16) f...  12.1 us
    ppermute x1, starting transfers between devices, per_device(): other = lax.ppermute(other, 'col', [(c, (c + 8) % 16) for c in range(16)])  3.32 us
  transfers between devices with their start and end apart: 1, of which 0 were waited for; matrix products, arithmetic and copies ran while one was open for 0% of the time, Pallas kernels for 8%

profile of v4, /device:TPU:0, one launch (start us, length us, event | category | flops | bytes accessed | tf_op | source)
XLA Modules:
  0.0 142.1 jit_solution(3391406875537156950)
XLA Ops:
  0.6 125.3 %exchange.1 = (bf16[2,768,1024]{2,1,0:T(8,128)(2,1)}, bf16[3,768,1664]{2,1,0:T(8,128)(2,1)}, f32[48,1024]{1,0:T(8,128)}, f32[48,1024]{1,0:T(8,128)}) custom-call(bf16[48,1024]{1,0:T(8,128)(2,1)} %act_in.1, bf16[48,1024]{1,0:T(8,128)(2,1)} %grad_in.1, bf16[1024,1664]{1,0:T(8,128)(2,1)} %wg_in.1, bf16[1024,1664]{1,0:T(8,128)(2,1)} %wu_in.1, ...), custom_call_target="tpu_custom_call" | custom-call | flops 13086228480 | bytes 23068672 | tf_op jit(solution)/shard_map/exchange/pallas_call | solution.py:501
  126.0 3.3 %collective-permute-start = (f32[48,1024]{1,0:T(8,128)}, f32[48,1024]{1,0:T(8,128)S(1)}, u32[]{:S(2)}, u32[]{:S(2)}) collective-permute-start(f32[48,1024]{1,0:T(8,128)} %get-tuple-element.12), channel_id=1, source_target_pairs={{0,8},{1,9},{2,10},{3,11},{4,12},{5,13},{6,14},{7,15},{8,0},{9,1},... | collective-permute-start | bytes 589832 | tf_op jit(solution)/shard_map/ppermute | solution.py:613
  129.3 0.0 copy-start
  129.3 12.1 %weight_grads.1 = (bf16[1024,1664]{1,0:T(8,128)(2,1)}, bf16[1024,1664]{1,0:T(8,128)(2,1)}, bf16[1664,1024]{1,0:T(8,128)(2,1)}) custom-call(bf16[2,768,1024]{2,1,0:T(8,128)(2,1)} %get-tuple-element.13.tok_in, bf16[3,768,1664]{2,1,0:T(8,128)(2,1)} %get-tuple-element.14.delta_in), custom_call_target="tpu_custom_call" | custom-call | flops 7851737088 | bytes 23068672 | tf_op jit(solution)/shard_map/weight_grads/pallas_call | solution.py:591
  141.4 0.0 collective-permute-done
  141.4 0.0 copy-done
  141.4 0.7 add_convert_fusion
Async XLA Ops:
  126.0 15.4 %collective-permute-start = (f32[48,1024]{1,0:T(8,128)}, f32[48,1024]{1,0:T(8,128)S(1)}, u32[]{:S(2)}, u32[]{:S(2)}) collective-permute-start(f32[48,1024]{1,0:T(8,128)} %get-tuple-element.12), channel_id=1, source_target_pairs={{0,8},{1,9},{2,10},{3,11},{4,12},{5,13},{6,14},{7,15},{8,0},{9,1},... | collective-permute-start | bytes 589832 | tf_op jit(solution)/shard_map/ppermute | solution.py:613
  129.3 12.1 %copy-start = (f32[48,1024]{1,0:T(8,128)S(1)}, f32[48,1024]{1,0:T(8,128)}, u32[]{:S(2)}) copy-start(f32[48,1024]{1,0:T(8,128)} %get-tuple-element.11) | copy-start | bytes 589828

commit v5 on v4

--- a/solution.py
+++ b/solution.py
@@ -223,7 +223,8 @@
 
     def gather_by(c, k, y_):
         sem = (gby_s.at[c, k], gby_r.at[c, k])
-        rows = (rows_b(c, y_, 0, 32), rows_b(c, y_, 0, 32), rows_b(c, y_, OWN, OWN), rows_b(c, y_, 0, OWN))[k]
+        mine, pair = rows_b(c, y_, OWN * zl, OWN), rows_b(c, y_, OWN * (1 - zl), OWN)
+        rows = (mine, mine, rows_b(c, y_, OWN, OWN), rows_b(c, y_, 0, OWN), pair, pair)[k]
         return same(delta_b.at[:, rows], *sem, down_y if k % 2 else up_y)
 
     def out_copies(c):
@@ -341,6 +342,8 @@
         for i, value in enumerate(swiglu_back(*sums)):
             delta_b[i, rows_b(c, y, OWN * zl, OWN), :] = value
         gather_bz(c, zl).start()
+        for k in range(2):
+            gather_by(c, k, y).start()
 
     def forward_a(c):
         gather_ay(c, 0, y_prev).wait_recv()
@@ -352,7 +355,7 @@
 
     def quarter_b(c):
         gather_bz(c, 1 - zl).wait_recv()
-        for k in range(2):
+        for k in (4, 5):
             gather_by(c, k, y).start()
 
     def swap_a(c):
@@ -361,9 +364,11 @@
         gather_az(c, 3, zl).start()
 
     def forward_b(c):
-        gather_by(c, 0, y_prev).wait_recv()
+        for k in (0, 4):
+            gather_by(c, k, y_prev).wait_recv()
         gather_by(c, 2, y_prev).start()
-        gather_by(c, 1, y_next).wait_recv()
+        for k in (1, 5):
+            gather_by(c, k, y_next).wait_recv()
         gather_by(c, 3, y_next).start()
 
     def input_grad_a(c):
@@ -486,6 +491,7 @@
             by(c, k).wait_send()
         for k in range(4):
             gather_ay(c, k, y).wait_send()
+        for k in range(6):
             gather_by(c, k, y).wait_send()
         for copy in out_copies(c):
             copy.wait()
@@ -533,7 +539,7 @@
             dma((7,)), dma((2,)), dma((2,)), dma((2, 8)), dma((2, 8)), dma((2, 6)), dma((2, 6)),
             dma((n, 3)), dma((n, 3)), dma((n,)), dma((n,)), dma((n, 4)), dma((n, 4)), dma((n,)), dma((n,)),
             dma((n, 6)), dma((n, 6)), dma((n, 6)), dma((n, 6)),
-            dma((n, 4)), dma((n, 4)), dma((n, 4)), dma((n, 4)),
+            dma((n, 4)), dma((n, 4)), dma((n, 6)), dma((n, 6)),
             dma((8,)), dma((8,)), dma((6,)), dma((6,)),
             dma((2, n)),
         ],

time: 142 us -> 142 us (level)
  transfers between devices with their start and end apart: 1 -> 1, of which waited for: 0 -> 0; matrix products, arithmetic and copies ran while one was open for 0% -> 0% of each run, Pallas kernels for 8% -> 9%
where the time goes in v5:
time: 142 us; the launch traced here: 141 us
  Pallas kernels  137 us (96%)
  starting transfers between devices  2.75 us (2%)
    pallas_call x1, Pallas kernels, exchange(): pl.pallas_call(exchange_kernel, out_shape=[jax.ShapeDtypeStruct((2, TOKEN...  125 us
    pallas_call x1, Pallas kernels, weight_grads(): pl.pallas_call(weights_kernel, out_shape=[jax.ShapeDtypeStruct(s, BF16) f...  12.1 us
  transfers between devices with their start and end apart: 1, of which 0 were waited for; matrix products, arithmetic and copies ran while one was open for 0% of the time, Pallas kernels for 9%

profile of v5, /device:TPU:0, one launch (start us, length us, event | category | flops | bytes accessed | tf_op | source)
XLA Modules:
  0.0 141.2 jit_solution(11321596339641605073)
XLA Ops:
  0.6 125.0 %exchange.1 = (bf16[2,768,1024]{2,1,0:T(8,128)(2,1)}, bf16[3,768,1664]{2,1,0:T(8,128)(2,1)}, f32[48,1024]{1,0:T(8,128)}, f32[48,1024]{1,0:T(8,128)}) custom-call(bf16[48,1024]{1,0:T(8,128)(2,1)} %act_in.1, bf16[48,1024]{1,0:T(8,128)(2,1)} %grad_in.1, bf16[1024,1664]{1,0:T(8,128)(2,1)} %wg_in.1, bf16[1024,1664]{1,0:T(8,128)(2,1)} %wu_in.1, ...), custom_call_target="tpu_custom_call" | custom-call | flops 13086228480 | bytes 23068672 | tf_op jit(solution)/shard_map/exchange/pallas_call | solution.py:507
  125.7 2.7 %collective-permute-start = (f32[48,1024]{1,0:T(8,128)}, f32[48,1024]{1,0:T(8,128)S(1)}, u32[]{:S(2)}, u32[]{:S(2)}) collective-permute-start(f32[48,1024]{1,0:T(8,128)} %get-tuple-element.12), channel_id=1, source_target_pairs={{0,8},{1,9},{2,10},{3,11},{4,12},{5,13},{6,14},{7,15},{8,0},{9,1},... | collective-permute-start | bytes 589832 | tf_op jit(solution)/shard_map/ppermute | solution.py:619
  128.4 0.0 copy-start
  128.4 12.1 %weight_grads.1 = (bf16[1024,1664]{1,0:T(8,128)(2,1)}, bf16[1024,1664]{1,0:T(8,128)(2,1)}, bf16[1664,1024]{1,0:T(8,128)(2,1)}) custom-call(bf16[2,768,1024]{2,1,0:T(8,128)(2,1)} %get-tuple-element.13.tok_in, bf16[3,768,1664]{2,1,0:T(8,128)(2,1)} %get-tuple-element.14.delta_in), custom_call_target="tpu_custom_call" | custom-call | flops 7851737088 | bytes 23068672 | tf_op jit(solution)/shard_map/weight_grads/pallas_call | solution.py:597
  140.5 0.0 collective-permute-done
  140.5 0.0 copy-done
  140.5 0.7 add_convert_fusion
Async XLA Ops:
  125.7 14.8 %collective-permute-start = (f32[48,1024]{1,0:T(8,128)}, f32[48,1024]{1,0:T(8,128)S(1)}, u32[]{:S(2)}, u32[]{:S(2)}) collective-permute-start(f32[48,1024]{1,0:T(8,128)} %get-tuple-element.12), channel_id=1, source_target_pairs={{0,8},{1,9},{2,10},{3,11},{4,12},{5,13},{6,14},{7,15},{8,0},{9,1},... | collective-permute-start | bytes 589832 | tf_op jit(solution)/shard_map/ppermute | solution.py:619
  128.4 12.1 %copy-start = (f32[48,1024]{1,0:T(8,128)S(1)}, f32[48,1024]{1,0:T(8,128)}, u32[]{:S(2)}) copy-start(f32[48,1024]{1,0:T(8,128)} %get-tuple-element.11) | copy-start | bytes 589828

commit v6 on v4

--- a/solution.py
+++ b/solution.py
@@ -314,9 +314,9 @@
         ]
         for i, value in enumerate(swiglu_back(*sums)):
             delta_a[i, rows_a(c, y), :] = value
+        gather_az(c, 0, zl).start()
         for k in range(2):
             gather_ay(c, k, y).start()
-        gather_az(c, 0, zl).start()
 
     def own_b(c):
         p = lax.rem(c, SLOTS)

time: 142 us -> 142 us (level)
  no operation moved by 1% of the time
where the time goes in v6:
time: 142 us
  Pallas kernels  137 us (96%)
  starting transfers between devices  3.32 us (2%)
    pallas_call x1, Pallas kernels, exchange(): pl.pallas_call(exchange_kernel, out_shape=[jax.ShapeDtypeStruct((2, TOKEN...  125 us
    pallas_call x1, Pallas kernels, weight_grads(): pl.pallas_call(weights_kernel, out_shape=[jax.ShapeDtypeStruct(s, BF16) f...  12.1 us
    ppermute x1, starting transfers between devices, per_device(): other = lax.ppermute(other, 'col', [(c, (c + 8) % 16) for c in range(16)])  3.32 us
  transfers between devices with their start and end apart: 1, of which 0 were waited for; matrix products, arithmetic and copies ran while one was open for 0% of the time, Pallas kernels for 8%

profile of v6, /device:TPU:0, one launch (start us, length us, event | category | flops | bytes accessed | tf_op | source)
XLA Modules:
  0.0 142.1 jit_solution(8615102848485963530)
XLA Ops:
  0.6 125.3 %exchange.1 = (bf16[2,768,1024]{2,1,0:T(8,128)(2,1)}, bf16[3,768,1664]{2,1,0:T(8,128)(2,1)}, f32[48,1024]{1,0:T(8,128)}, f32[48,1024]{1,0:T(8,128)}) custom-call(bf16[48,1024]{1,0:T(8,128)(2,1)} %act_in.1, bf16[48,1024]{1,0:T(8,128)(2,1)} %grad_in.1, bf16[1024,1664]{1,0:T(8,128)(2,1)} %wg_in.1, bf16[1024,1664]{1,0:T(8,128)(2,1)} %wu_in.1, ...), custom_call_target="tpu_custom_call" | custom-call | flops 13086228480 | bytes 23068672 | tf_op jit(solution)/shard_map/exchange/pallas_call | solution.py:501
  126.0 3.3 %collective-permute-start = (f32[48,1024]{1,0:T(8,128)}, f32[48,1024]{1,0:T(8,128)S(1)}, u32[]{:S(2)}, u32[]{:S(2)}) collective-permute-start(f32[48,1024]{1,0:T(8,128)} %get-tuple-element.12), channel_id=1, source_target_pairs={{0,8},{1,9},{2,10},{3,11},{4,12},{5,13},{6,14},{7,15},{8,0},{9,1},... | collective-permute-start | bytes 589832 | tf_op jit(solution)/shard_map/ppermute | solution.py:613
  129.3 0.0 copy-start
  129.3 12.1 %weight_grads.1 = (bf16[1024,1664]{1,0:T(8,128)(2,1)}, bf16[1024,1664]{1,0:T(8,128)(2,1)}, bf16[1664,1024]{1,0:T(8,128)(2,1)}) custom-call(bf16[2,768,1024]{2,1,0:T(8,128)(2,1)} %get-tuple-element.13.tok_in, bf16[3,768,1664]{2,1,0:T(8,128)(2,1)} %get-tuple-element.14.delta_in), custom_call_target="tpu_custom_call" | custom-call | flops 7851737088 | bytes 23068672 | tf_op jit(solution)/shard_map/weight_grads/pallas_call | solution.py:591
  141.4 0.0 collective-permute-done
  141.4 0.0 copy-done
  141.4 0.7 add_convert_fusion
Async XLA Ops:
  126.0 15.4 %collective-permute-start = (f32[48,1024]{1,0:T(8,128)}, f32[48,1024]{1,0:T(8,128)S(1)}, u32[]{:S(2)}, u32[]{:S(2)}) collective-permute-start(f32[48,1024]{1,0:T(8,128)} %get-tuple-element.12), channel_id=1, source_target_pairs={{0,8},{1,9},{2,10},{3,11},{4,12},{5,13},{6,14},{7,15},{8,0},{9,1},... | collective-permute-start | bytes 589832 | tf_op jit(solution)/shard_map/ppermute | solution.py:613
  129.3 12.1 %copy-start = (f32[48,1024]{1,0:T(8,128)S(1)}, f32[48,1024]{1,0:T(8,128)}, u32[]{:S(2)}) copy-start(f32[48,1024]{1,0:T(8,128)} %get-tuple-element.11) | copy-start | bytes 589828
